TPU v7x, 128 devices: a whole 4x4x4 slice. The times are simulated.
128 devices in a mesh: row: 8 (over y_hi, z), col: 16 (over y_lo, x, core).
Axes of the slice: x: 4, y: 4 (y_hi: 2, y_lo: 2; y = y_hi * 2 + y_lo), z: 4, core: 2. Of those that a mesh axis runs over, the one named last changes fastest.
Arguments:
- left_tiles: bfloat16 [32, 4096, 256], P('row', 'col'), may hold values from 0.00049972534 to 0.049804688
- left_slots: int32 [32, 16], P('row', 'col'), may hold values from -1 to 7, as said below
- right_tiles: bfloat16 [32, 4096, 256], P('row', 'col'), may hold values from 0.00049972534 to 0.049804688
- right_slots: int32 [32, 16], P('row', 'col'), may hold values from -1 to 7, as said below
Outputs:
- inflated: float32 [16384, 16384], P('row', 'col')
Inputs may be any that keep to these rules, and one draw needn't show every extreme that they name: `left_slots`: in each device's 4 slots the entries that are not -1 are distinct; half of the slots or more hold a tile, and some device holds a tile in every slot. `right_slots`: in each device's 4 slots the entries that are not -1 are distinct; half of the slots or more hold a tile, and some device holds a tile in every slot.
All inputs are finite; a program needn't handle non-finite values.
Results may differ from a plain program's by a relative error of at most 0.0003.
Values may be sent and summed in bfloat16 or wider, within the bound.
A program may use at most 192 MiB of HBM per device.

v0:
```python
import jax
import jax.numpy as jnp
from jax import lax
from jax.sharding import PartitionSpec as P

TILE = 256
RB_DEV = 8
CB_DEV = 4
KB_DEV = 1


EPSILON = 1e-06


def densify(tile_set, slot_ids, dense_count):
    slot_total = tile_set.shape[0]
    matches = slot_ids[:, 0][None, :] == jnp.arange(dense_count, dtype=jnp.int32)[:, None]
    which_slot = jnp.sum(
        jnp.where(matches, jnp.arange(slot_total, dtype=jnp.int32)[None, :], 0), axis=1
    )
    present = jnp.any(matches, axis=1)
    return jnp.where(present[:, None, None], tile_set[which_slot], jnp.zeros((), tile_set.dtype))


def body(left_tiles, left_slots, right_tiles, right_slots):
    n_row = lax.axis_size("row")
    n_col = lax.axis_size("col")
    inner_local = KB_DEV * n_col // n_row
    right_dense = densify(right_tiles, right_slots, inner_local * CB_DEV)
    right_matrix = right_dense.reshape(inner_local, CB_DEV, TILE, TILE).transpose(0, 2, 1, 3)
    right_matrix = right_matrix.reshape(inner_local * TILE, CB_DEV * TILE)
    right_whole = lax.all_gather(right_matrix, "row", axis=0, tiled=True)
    left_dense = densify(left_tiles, left_slots, RB_DEV * KB_DEV)
    left_matrix = left_dense.reshape(RB_DEV, KB_DEV, TILE, TILE).transpose(0, 2, 1, 3)
    left_matrix = left_matrix.reshape(RB_DEV * TILE, KB_DEV * TILE)
    expanded = jnp.dot(
        lax.all_gather(left_matrix, "col", axis=1, tiled=True),
        right_whole,
        preferred_element_type=jnp.float32,
    )
    squared = expanded * expanded
    col_part = jnp.sum(squared, axis=0)
    col_total = lax.psum(col_part, "row")
    rows_all = RB_DEV * TILE * n_row
    return squared / (col_total / rows_all + EPSILON)


def solution(mesh):
    placed = (P("row", "col", None), P("row", "col"), P("row", "col", None), P("row", "col"))
    return jax.shard_map(
        body, mesh=mesh, in_specs=placed, out_specs=P("row", "col"), check_vma=False
    )
```

profile of v0, /device:TPU:0, one launch (start us, length us, event | category | flops | bytes accessed | tf_op | source)
XLA Modules:
  0.0 283.2 jit_solution(16809381194892955468)
XLA Ops:
  6.5 0.0 copy-start
  6.5 0.0 all-gather.5.cloned.1.call-start
  6.5 0.8 select_reduce_fusion
  7.3 0.7 fusion
  8.1 0.1 broadcast_in_dim.59
  8.2 0.0 copy-done
  8.2 0.6 gather_fusion.1
  8.8 0.8 copy_select_fusion
  9.7 1.3 copy.7
  11.0 0.0 all-gather.5.cloned.1.call-update
  11.0 0.0 all-gather.3.cloned.1.call-start
  11.0 0.7 fusion.1
  11.8 0.1 broadcast_in_dim.53
  11.9 0.7 select_reduce_fusion.1
  12.6 1.7 gather_fusion
  14.3 1.3 bitcast_select_fusion
  15.6 0.0 all-gather.3.cloned.1.call-update
  15.6 105.2 %all-gather.5.cloned.1.call-done = bf16[4096,1024]{1,0:T(8,128)(2,1)} async-done(((bf16[512,1024]{1,0:T(8,128)(2,1)}), bf16[4096,1024]{1,0:T(8,128)(2,1)}) %all-gather.5.cloned.1.call-update) | async-done | bytes 8388624 | tf_op jit(solution)/shard_map/all_gather | solution.py:32
  120.9 98.4 %all-gather.3.cloned.1.call-done = bf16[2048,4096]{1,0:T(8,128)(2,1)} async-done(((bf16[2048,256]{1,0:T(8,128)(2,1)}), bf16[2048,4096]{1,0:T(8,128)(2,1)}) %all-gather.3.cloned.1.call-update) | async-done | bytes 16777232 | tf_op jit(solution)/shard_map/all_gather | solution.py:37
  219.3 24.0 %multiply_reduce_fusion = (f32[1024]{0:T(1024)S(1)}, f32[2048,1024]{1,0:T(8,128)}) fusion(bf16[2048,4096]{1,0:T(8,128)(2,1)} %all-gather.3.cloned.1.call-done, bf16[4096,1024]{1,0:T(8,128)(2,1)} %all-gather.5.cloned.1.call-done), kind=kOutput, calls=%fused_computation.3 | convolution fusion | flops 17184063488 | bytes 33558528 | tf_op jit(solution)/shard_map/dot_general | solution.py:36
  243.3 24.3 %psum.7 = f32[1024]{0:T(1024)S(1)} all-reduce(f32[1024]{0:T(1024)S(1)} %get-tuple-element.5), channel_id=1, replica_groups=mesh['row'=8,'col'=16] {'row'}, use_global_device_ids=true, to_apply=%region_5.6 | all-reduce | flops 1024 | bytes 8192 | tf_op jit(solution)/shard_map/psum | solution.py:43
  267.6 8.8 %multiply_divide_fusion = f32[2048,1024]{1,0:T(8,128)} fusion(f32[2048,1024]{1,0:T(8,128)} %get-tuple-element.6, f32[1024]{0:T(1024)S(1)} %multiply_add_fusion), kind=kLoop, calls=%fused_computation.2 | loop fusion | flops 4194304 | bytes 16781312 | tf_op jit(solution)/shard_map/div | solution.py:45
  (6 shorter events, 0.0 us)
Async XLA Ops:
  6.5 1.6 copy-start
  6.5 114.3 %all-gather.5.cloned.1.call-start = ((), (), s32[]{:S(2)}) async-start(), calls=%async_computation.1 | async-start | bytes 9437184 | tf_op jit(solution)/shard_map/all_gather | solution.py:32
  11.0 208.3 %all-gather.3.cloned.1.call-start = ((), (), s32[]{:S(2)}) async-start(), calls=%async_computation | async-start | bytes 17825792 | tf_op jit(solution)/shard_map/all_gather | solution.py:37
Sparse Core Ops, SparseCore 0:
  11.1 109.7 all-gather.4
  122.5 96.7 all-gather.2
where the time goes:
time: 283 us
  waiting for transfers between devices  204 us (72%)
  blocking collectives  24.3 us (9%)
  matrix products  24 us (8%)
  other arithmetic  14 us (5%)
  between operations  13.4 us (5%)
  local copies, waits for them, and re-layouts  3.74 us (1%)
    all_gather x1, waiting for transfers between devices, body(): right_whole = lax.all_gather(right_matrix, 'row', axis=0, tiled=True)  105 us
    all_gather x1, waiting for transfers between devices, body(): lax.all_gather(left_matrix, 'col', axis=1, tiled=True)  98.4 us
    psum x1, blocking collectives, body(): col_total = lax.psum(col_part, 'row')  24.3 us
    dot_general x1, matrix products, body(): jnp.dot(lax.all_gather(left_matrix, 'col', axis=1, tiled=True), right_who...  24 us
    div x1, other arithmetic, body(): return squared / (col_total / rows_all + EPSILON)  8.79 us
  transfers between devices with their start and end apart: 2, of which 2 were waited for; matrix products, arithmetic and copies ran while one was open for 2% of the time, Pallas kernels for 0%

commit v1 on v0

v1 whole, which is shorter than its diff:
```python
import functools

import jax
import jax.numpy as jnp
from jax import lax
from jax.experimental import pallas as pl
from jax.experimental.pallas import tpu as pltpu
from jax.sharding import PartitionSpec as P

TILE = 256
RB_DEV = 8
CB_DEV = 4
CAP = 4
N_ROW = 8
N_COL = 16
SLAB = CAP * TILE
LANES = 128
EPSILON = 1e-06
MESH = pl.DeviceIdType.MESH
ANY = pl.BlockSpec(memory_space=pl.ANY)
VMEM = pl.BlockSpec(memory_space=pltpu.VMEM)
SMEM = pl.BlockSpec(memory_space=pltpu.SMEM)


class Factor:
    def __init__(self, out, own, place, device, send, recv, sibling):
        self.out, self.own, self.place, self.device = out, own, place, device
        self.send, self.recv, self.sibling = send, recv, sibling
        self.sent, self.count = [], 0

    def tile(self, slab, q):
        return self.out.at[self.place(*slab), pl.ds(q * TILE, TILE)]

    def start(self, slab, q, ring, pair):
        there = ((slab[0] - ring) % 4, (slab[1] - pair) % 2)
        source = self.own.at[pl.ds(q * TILE, TILE)] if slab == (0, 0) else self.tile(slab, q)
        copy = pltpu.make_async_remote_copy(
            src_ref=source,
            dst_ref=self.tile(slab, q),
            send_sem=self.send.at[self.count],
            recv_sem=self.recv.at[(there[0] + 4 * there[1]) * 4 + q],
            device_id=self.device(ring, pair),
            device_id_type=MESH,
        )
        copy.start()
        self.count += 1
        self.sent.append(copy)

    def arrived(self, slab, q):
        here = self.tile(slab, q)
        pltpu.make_async_copy(here, here, self.recv.at[(slab[0] + 4 * slab[1]) * 4 + q]).wait()
        if self.sibling is not None:
            self.sibling(self, slab, q)

    def begin(self, step):
        self.start((0, 0), (0, 3, 1, 2)[step], 0, 1)
        self.start((0, 0), step, 1, 0)
        self.start((0, 0), 3 - step, 3, 0)

    def events(self):
        def ring(pair, q, forward):
            def run():
                self.arrived((3, pair), q)
                if forward:
                    self.start((3, pair), q, 1, 0)
                self.arrived((1, pair), 3 - q)
                if forward:
                    self.start((1, pair), 3 - q, 3, 0)
            return run

        def across(q):
            def run():
                self.arrived((0, 1), q)
                self.start((0, 1), q, 1, 0)
                self.start((0, 1), q, 3, 0)
            return run

        def both(q, up, down):
            def run():
                self.arrived((3, 1), q)
                if up:
                    self.start((3, 1), q, 1, 0)
                self.arrived((1, 1), q)
                if down:
                    self.start((1, 1), q, 3, 0)
            return run

        def far(pair, q):
            def run():
                self.arrived((2, pair), q)
                self.arrived((2, pair), 3 - q)
            return run

        return [
            ring(0, 0, True), ring(0, 1, True), across(0), ring(0, 2, False), ring(0, 3, False),
            across(3), far(0, 0), far(0, 1), across(1), both(0, True, False), both(3, False, True),
            across(2), both(1, True, False), both(2, False, True), far(1, 0), far(1, 1),
        ]


def gather_kernel(left, right, left_slots, right_slots, left_all, right_all, left_ids, right_ids,
                  ids, left_send, left_recv, right_send, right_recv, sib_send, sib_recv,
                  idl_send, idl_recv, idr_send, idr_recv, own_sem):
    row, col = lax.axis_index("row"), lax.axis_index("col")
    y_hi, z = row // 4, lax.rem(row, 4)
    core, x, y_lo = lax.rem(col, 2), lax.rem(col // 2, 4), col // 8

    def left_place(ring, pair):
        return (lax.rem(y_lo + pair, 2) * 4 + lax.rem(x + ring, 4)) * 2 + core

    def right_place(ring, pair):
        return lax.rem(y_hi + pair, 2) * 4 + lax.rem(z + ring, 4)

    other = (row, col + 1 - 2 * core)

    barrier = pltpu.get_barrier_semaphore()
    for step in range(1, N_COL):
        pl.semaphore_signal(barrier, inc=1, device_id=(row, lax.rem(col + step, N_COL)), device_id_type=MESH)
    for step in range(1, N_ROW):
        pl.semaphore_signal(barrier, inc=1, device_id=(lax.rem(row + step, N_ROW), col), device_id_type=MESH)

    lane = lax.broadcasted_iota(jnp.int32, (1, LANES), 1)
    row_ids = jnp.full((1, LANES), -1, jnp.int32)
    for s in range(CAP):
        row_ids = jnp.where(lane == s, left_slots[s, 0], row_ids)
        row_ids = jnp.where(lane == CAP + s, right_slots[s, 0], row_ids)
    ids[...] = row_ids

    pl.semaphore_wait(barrier, N_COL + N_ROW - 2)

    shared = []

    def to_sibling(factor, slab, q):
        index = (slab[0] + 4 * slab[1]) * 4 + q
        part = factor.tile(slab, q)
        copy = pltpu.make_async_remote_copy(
            src_ref=factor.own.at[pl.ds(q * TILE, TILE)] if slab == (0, 0) else part,
            dst_ref=part,
            send_sem=sib_send.at[index],
            recv_sem=sib_recv.at[index],
            device_id=other,
            device_id_type=MESH,
        )
        copy.start()
        shared.append(copy)

    lf = Factor(left_all, left, left_place, lambda ring, pair: (row, left_place(ring, pair)), left_send, left_recv, to_sibling)
    rf = Factor(right_all, right, right_place, lambda ring, pair: (right_place(ring, pair), col), right_send, right_recv, None)

    for step in range(4):
        lf.begin(step)
        rf.begin(step)

    small = []
    for step in range(1, N_COL):
        copy = pltpu.make_async_remote_copy(
            src_ref=ids, dst_ref=left_ids.at[col], send_sem=idl_send.at[step], recv_sem=idl_recv.at[step],
            device_id=(row, lax.rem(col + step, N_COL)), device_id_type=MESH)
        copy.start()
        small.append(copy)
    for step in range(1, N_ROW):
        copy = pltpu.make_async_remote_copy(
            src_ref=ids, dst_ref=right_ids.at[row], send_sem=idr_send.at[step], recv_sem=idr_recv.at[step],
            device_id=(lax.rem(row + step, N_ROW), col), device_id_type=MESH)
        copy.start()
        small.append(copy)
    for q in range(CAP):
        to_sibling(lf, (0, 0), q)
    local = [
        pltpu.make_async_copy(left, left_all.at[col], own_sem.at[0]),
        pltpu.make_async_copy(right, right_all.at[row], own_sem.at[1]),
        pltpu.make_async_copy(ids, left_ids.at[col], own_sem.at[2]),
        pltpu.make_async_copy(ids, right_ids.at[row], own_sem.at[3]),
    ]
    for copy in local:
        copy.start()

    for left_event, right_event in zip(lf.events(), rf.events()):
        left_event()
        right_event()

    for copy in local:
        copy.wait()
    for index in range(8 * CAP):
        ring, pair, q = index // 4 % 4, index // 16, index % 4
        place = left_place(ring, pair) + 1 - 2 * core
        part = left_all.at[place, pl.ds(q * TILE, TILE)]
        pltpu.make_async_copy(part, part, sib_recv.at[index]).wait()
    for copy in small:
        copy.wait_recv()
    for copy in small + shared + lf.sent + rf.sent:
        copy.wait_send()


def gather(left, right, left_slots, right_slots):
    dma = pltpu.SemaphoreType.DMA
    return pl.pallas_call(
        gather_kernel,
        out_shape=[
            KEEP((N_COL, SLAB, TILE), jnp.bfloat16),
            KEEP((N_ROW, SLAB, TILE), jnp.bfloat16),
            jax.ShapeDtypeStruct((N_COL, 1, LANES), jnp.int32),
            jax.ShapeDtypeStruct((N_ROW, 1, LANES), jnp.int32),
        ],
        in_specs=[ANY, ANY, SMEM, SMEM],
        out_specs=[KEEP_SPEC, KEEP_SPEC, ANY, ANY],
        scratch_shapes=[
            pltpu.VMEM((1, LANES), jnp.int32),
            dma((28,)), dma((32,)), dma((28,)), dma((32,)), dma((32,)), dma((32,)),
            dma((N_COL,)), dma((N_COL,)), dma((N_ROW,)), dma((N_ROW,)), dma((4,)),
        ],
        compiler_params=pltpu.CompilerParams(collective_id=0, has_side_effects=True),
        name="gather_slabs",
    )(left, right, left_slots, right_slots)


def product_kernel(left_ids, right_ids, left_all, right_all, expanded, col_part):
    expanded[...] = jnp.zeros_like(expanded)

    def inner(k, _):
        for s in range(CAP):
            held = right_ids[k // 2, 0, CAP + s]

            @pl.when((held >= 0) & (held // CB_DEV == lax.rem(k, 2)))
            def _():
                j = lax.rem(held, CB_DEV)
                weights = right_all[k // 2, pl.ds(s * TILE, TILE)]
                for u in range(CAP):
                    i = left_ids[k, 0, u]

                    @pl.when(i >= 0)
                    def _():
                        part = jnp.dot(left_all[k, pl.ds(u * TILE, TILE)], weights, preferred_element_type=jnp.float32)
                        at = (pl.ds(pl.multiple_of(i * TILE, TILE), TILE), pl.ds(pl.multiple_of(j * TILE, TILE), TILE))
                        expanded[at] += part
        return 0

    lax.fori_loop(0, N_COL, inner, 0)

    def add(i, total):
        part = expanded[pl.ds(pl.multiple_of(i * 64, 64), 64)]
        return total + jnp.sum((part * part).reshape(8, 8, CB_DEV * TILE), axis=0)

    total = lax.fori_loop(0, RB_DEV * TILE // 64, add, jnp.zeros((8, CB_DEV * TILE), jnp.float32))
    col_part[...] = jnp.sum(total, axis=0, keepdims=True)


def product(left_ids, right_ids, left_all, right_all):
    return pl.pallas_call(
        product_kernel,
        out_shape=[
            KEEP((RB_DEV * TILE, CB_DEV * TILE), jnp.float32),
            jax.ShapeDtypeStruct((1, CB_DEV * TILE), jnp.float32),
        ],
        in_specs=[SMEM, SMEM, VMEM, VMEM],
        out_specs=[VMEM, VMEM],
        compiler_params=pltpu.CompilerParams(vmem_limit_bytes=24 * 2**20),
        name="tile_products",
    )(left_ids, right_ids, left_all, right_all)


def total_kernel(part, total, held, send, recv):
    row, col = lax.axis_index("row"), lax.axis_index("col")
    barrier = pltpu.get_barrier_semaphore()
    for step in range(1, N_ROW):
        pl.semaphore_signal(barrier, inc=1, device_id=(lax.rem(row + step, N_ROW), col), device_id_type=MESH)
    pl.semaphore_wait(barrier, N_ROW - 1)
    copies = []
    for step in range(1, N_ROW):
        copy = pltpu.make_async_remote_copy(
            src_ref=part, dst_ref=held.at[step], send_sem=send.at[step], recv_sem=recv.at[step],
            device_id=(lax.rem(row + step, N_ROW), col), device_id_type=MESH)
        copy.start()
        copies.append(copy)
    value = part[...]
    for step, copy in enumerate(copies):
        copy.wait_recv()
        value = value + held[step + 1]
    total[...] = value
    for copy in copies:
        copy.wait_send()


def column_total(part):
    dma = pltpu.SemaphoreType.DMA
    return pl.pallas_call(
        total_kernel,
        out_shape=jax.ShapeDtypeStruct(part.shape, part.dtype),
        in_specs=[VMEM],
        out_specs=VMEM,
        scratch_shapes=[pltpu.VMEM((N_ROW, *part.shape), part.dtype), dma((N_ROW,)), dma((N_ROW,))],
        compiler_params=pltpu.CompilerParams(collective_id=1, has_side_effects=True),
        name="column_total",
    )(part)


def scale_kernel(total, expanded, out):
    factor = 1.0 / (total[...] / (RB_DEV * TILE * N_ROW) + EPSILON)
    value = expanded[...]
    out[...] = value * value * factor


def scale(total, expanded):
    rows, cols = expanded.shape
    step = 256
    return pl.pallas_call(
        scale_kernel,
        grid=(rows // step,),
        out_shape=jax.ShapeDtypeStruct(expanded.shape, jnp.float32),
        in_specs=[pl.BlockSpec((1, cols), lambda i: (0, 0)), pl.BlockSpec((step, cols), lambda i: (i, 0))],
        out_specs=pl.BlockSpec((step, cols), lambda i: (i, 0)),
        name="scale_columns",
    )(total, expanded)


KEEP = jax.ShapeDtypeStruct
KEEP_SPEC = ANY


def body(left_tiles, left_slots, right_tiles, right_slots):
    left = left_tiles.reshape(SLAB, TILE)
    right = right_tiles.reshape(SLAB, TILE)
    left_all, right_all, left_ids, right_ids = gather(left, right, left_slots, right_slots)
    expanded, col_part = product(left_ids, right_ids, left_all, right_all)
    return scale(column_total(col_part), expanded)


def solution(mesh):
    placed = (P("row", "col", None), P("row", "col"), P("row", "col", None), P("row", "col"))
    return jax.shard_map(
        body, mesh=mesh, in_specs=placed, out_specs=P("row", "col"), check_vma=False
    )
```

time: 283 us -> 102 us (0.36)
  waiting for transfers between devices: 204 us -> 0 us
  Pallas kernels: 0 us -> 88 us
  blocking collectives: 24.3 us -> 0 us
  matrix products: 24 us -> 0 us
  other arithmetic: 14 us -> 0 us
  between operations: 13.4 us -> 0.04 us
  local copies, waits for them, and re-layouts: 3.74 us -> 13.4 us
    all_gather x2 -> x0, waiting for transfers between devices: 204 us -> none  [the longest x1 105 us: body(): right_whole = lax.all_gather(right_matrix, 'row', axis=0, tiled=True)]
    pallas_call x0 -> x4, Pallas kernels: none -> 88 us  [the longest x1 49.8 us: gather(): pl.pallas_call(gather_kernel, out_shape=[KEEP((N_COL, SLAB, TILE), jnp.bf...]
    psum x1 -> x0, blocking collectives: 24.3 us -> none  [body(): col_total = lax.psum(col_part, 'row')]
    dot_general x1 -> x0, matrix products: 24 us -> none  [body(): jnp.dot(lax.all_gather(left_matrix, 'col', axis=1, tiled=True), right_who...]
    unnamed x3 -> x14, local copies, waits for them, and re-layouts: 1.3 us -> 13.4 us
    div x1 -> x0, other arithmetic: 8.79 us -> none  [body(): return squared / (col_total / rows_all + EPSILON)]
  transfers between devices with their start and end apart: 2 -> 0, of which waited for: 2 -> 0; matrix products, arithmetic and copies ran while one was open for 2% -> 0% of each run, Pallas kernels for 0% -> 0%
where the time goes in v1:
time: 102 us; the launch traced here: 101 us
  Pallas kernels  88 us (86%)
  local copies, waits for them, and re-layouts  13.4 us (13%)
    pallas_call x1, Pallas kernels, gather(): pl.pallas_call(gather_kernel, out_shape=[KEEP((N_COL, SLAB, TILE), jnp.bf...  49.8 us
    pallas_call x1, Pallas kernels, product(): pl.pallas_call(product_kernel, out_shape=[KEEP((RB_DEV * TILE, CB_DEV * T...  18.4 us
    unnamed x14, local copies, waits for them, and re-layouts  13.4 us
    pallas_call x1, Pallas kernels, column_total(): pl.pallas_call(total_kernel, out_shape=jax.ShapeDtypeStruct(part.shape, p...  10.7 us
    pallas_call x1, Pallas kernels, scale(): pl.pallas_call(scale_kernel, grid=(rows // step,), out_shape=jax.ShapeDty...  9.04 us

profile of v1, /device:TPU:0, one launch (start us, length us, event | category | flops | bytes accessed | tf_op | source)
XLA Modules:
  0.0 101.4 jit_solution(14205022045665704510)
XLA Ops:
  0.0 1.3 %copy.5.left_slots = s32[4,1]{1,0:T(4,128)} copy(s32[4,1]{0,1:T(1,128)} %param.5) | data formatting | bytes 32 | tf_op args[1]
  1.3 1.3 %copy.6.right_slots = s32[4,1]{1,0:T(4,128)} copy(s32[4,1]{0,1:T(1,128)} %param.7) | data formatting | bytes 32 | tf_op args[3]
  2.6 49.8 %gather_slabs.1 = (bf16[16,1024,256]{2,1,0:T(8,128)(2,1)}, bf16[8,1024,256]{2,1,0:T(8,128)(2,1)}, s32[16,1,128]{2,1,0:T(1,128)}, s32[8,1,128]{2,1,0:T(1,128)}) custom-call(bf16[1024,256]{1,0:T(8,128)(2,1)} %bitcast.2, bf16[1024,256]{1,0:T(8,128)(2,1)} %bitcast.3, s32[4,1]{1,0:T(4,128)} %copy.5.left_slots, s32[4,1]{1,0:T(4,128)} %copy.6.right_slots), custom_call_target="tpu_custom_call" | custom-call | tf_op jit(solution)/shard_map/gather_slabs/pallas_call | solution.py:197
  52.4 0.0 copy-start.1
  52.5 3.4 %copy-done.1 = bf16[16,1024,256]{2,1,0:T(8,128)(2,1)S(1)} copy-done((bf16[16,1024,256]{2,1,0:T(8,128)(2,1)S(1)}, bf16[16,1024,256]{2,1,0:T(8,128)(2,1)}, u32[]{:S(2)}) %copy-start.1) | copy-done | bytes 8388632
  55.8 0.0 copy-start.2
  55.8 2.2 %copy-done.2 = bf16[8,1024,256]{2,1,0:T(8,128)(2,1)S(1)} copy-done((bf16[8,1024,256]{2,1,0:T(8,128)(2,1)S(1)}, bf16[8,1024,256]{2,1,0:T(8,128)(2,1)}, u32[]{:S(2)}) %copy-start.2) | copy-done | bytes 4194328
  58.0 0.0 copy-start.3
  58.0 0.7 copy-done.3
  58.7 0.0 copy-start.4
  58.7 0.7 copy-done.4
  59.4 18.4 %tile_products.1 = (f32[2048,1024]{1,0:T(8,128)S(1)}, f32[1,1024]{1,0:T(1,128)S(1)}) custom-call(s32[16,1,128]{2,1,0:T(1,128)S(1)} %copy-done.3, s32[8,1,128]{2,1,0:T(1,128)S(1)} %copy-done.4, bf16[16,1024,256]{2,1,0:T(8,128)(2,1)S(1)} %copy-done.1, bf16[8,1024,256]{2,1,0:T(8,128)(2,1)S(1)} %copy-done.2), custom_call_target="tpu_custom_call" | custom-call | tf_op jit(solution)/shard_map/tile_products/pallas_call | solution.py:249
  77.8 0.0 copy-start
  77.8 3.2 %copy-done = f32[2048,1024]{1,0:T(8,128)} copy-done((f32[2048,1024]{1,0:T(8,128)}, f32[2048,1024]{1,0:T(8,128)S(1)}, u32[]{:S(2)}) %copy-start) | copy-done | bytes 8388632
  81.0 0.0 copy-start.5
  81.0 0.6 copy-done.5
  81.6 10.7 %column_total.1.total = f32[1,1024]{1,0:T(1,128)} custom-call(f32[1,1024]{1,0:T(1,128)} %copy-done.5), custom_call_target="tpu_custom_call" | custom-call | tf_op jit(solution)/shard_map/column_total/pallas_call | solution.py:286
  92.3 9.0 %scale_columns.1 = f32[2048,1024]{1,0:T(8,128)} custom-call(f32[1,1024]{1,0:T(1,128)} %column_total.1.total, f32[2048,1024]{1,0:T(8,128)} %copy-done), custom_call_target="tpu_custom_call" | custom-call | tf_op jit(solution)/shard_map/scale_columns/pallas_call | solution.py:306
Async XLA Ops:
  52.4 3.4 %copy-start.1 = (bf16[16,1024,256]{2,1,0:T(8,128)(2,1)S(1)}, bf16[16,1024,256]{2,1,0:T(8,128)(2,1)}, u32[]{:S(2)}) copy-start(bf16[16,1024,256]{2,1,0:T(8,128)(2,1)} %get-tuple-element.13.left_all) | copy-start | bytes 25165828
  55.8 2.2 %copy-start.2 = (bf16[8,1024,256]{2,1,0:T(8,128)(2,1)S(1)}, bf16[8,1024,256]{2,1,0:T(8,128)(2,1)}, u32[]{:S(2)}) copy-start(bf16[8,1024,256]{2,1,0:T(8,128)(2,1)} %get-tuple-element.14.right_all) | copy-start | bytes 12582916
  58.0 0.7 copy-start.3
  58.7 0.7 copy-start.4
  77.8 3.2 %copy-start = (f32[2048,1024]{1,0:T(8,128)}, f32[2048,1024]{1,0:T(8,128)S(1)}, u32[]{:S(2)}) copy-start(f32[2048,1024]{1,0:T(8,128)S(1)} %get-tuple-element.16.expanded) | copy-start | bytes 25165828
  81.0 0.6 copy-start.5

commit v2 on v1

v2 whole, which is shorter than its diff:
```python
import functools

import jax
import jax.numpy as jnp
from jax import lax
from jax.experimental import pallas as pl
from jax.experimental.pallas import tpu as pltpu
from jax.sharding import PartitionSpec as P

TILE = 256
RB_DEV = 8
CB_DEV = 4
CAP = 4
N_ROW = 8
N_COL = 16
SLAB = CAP * TILE
LANES = 128
EPSILON = 1e-06
MESH = pl.DeviceIdType.MESH
ANY = pl.BlockSpec(memory_space=pl.ANY)
VMEM = pl.BlockSpec(memory_space=pltpu.VMEM)
SMEM = pl.BlockSpec(memory_space=pltpu.SMEM)
HBM = pl.BlockSpec(memory_space=pltpu.HBM)


class Factor:
    UP = [((0, 0), q) for q in (0, 1, 2, 3)] + [((3, 0), 0), ((3, 0), 2)] + [((0, 1), q) for q in (0, 1, 2, 3)] + [((3, 1), 0), ((3, 1), 2)]
    DOWN = [((0, 0), q) for q in (1, 0, 3, 2)] + [((1, 0), 1), ((1, 0), 3)] + [((0, 1), q) for q in (1, 0, 2, 3)] + [((1, 1), 1), ((1, 1), 3)]
    TICKS = len(UP)
    WINDOW = 2

    def __init__(self, out, own, place, device, send, recv, sibling):
        self.out, self.own, self.place, self.device = out, own, place, device
        self.send, self.recv, self.sibling = send, recv, sibling
        self.count, self.here = 0, set()
        self.lines = {"up": [], "down": [], "pair": []}

    def tile(self, slab, q):
        return self.out.at[self.place(*slab), pl.ds(q * TILE, TILE)]

    def start(self, line, slab, q, ring, pair):
        sent = self.lines[line]
        if len(sent) >= self.WINDOW:
            sent[-self.WINDOW].wait_send()
        if slab != (0, 0):
            self.arrived(slab, q)
        there = ((slab[0] - ring) % 4, (slab[1] - pair) % 2)
        source = self.own.at[pl.ds(q * TILE, TILE)] if slab == (0, 0) else self.tile(slab, q)
        copy = pltpu.make_async_remote_copy(
            src_ref=source,
            dst_ref=self.tile(slab, q),
            send_sem=self.send.at[self.count],
            recv_sem=self.recv.at[(there[0] + 4 * there[1]) * 4 + q],
            device_id=self.device(ring, pair),
            device_id_type=MESH,
        )
        copy.start()
        self.count += 1
        sent.append(copy)

    def arrived(self, slab, q):
        if (slab, q) in self.here:
            return
        self.here.add((slab, q))
        here = self.tile(slab, q)
        pltpu.make_async_copy(here, here, self.recv.at[(slab[0] + 4 * slab[1]) * 4 + q]).wait()
        if self.sibling is not None:
            self.sibling(self, slab, q)

    def tick(self, t):
        if t % 2 == 0 and t // 2 < CAP:
            self.start("pair", (0, 0), t // 2, 0, 1)
        if t < self.TICKS:
            self.start("up", *self.UP[t], 1, 0)
            self.start("down", *self.DOWN[t], 3, 0)
        if 2 <= t < self.TICKS + 2:
            (ring, pair), q = self.UP[t - 2]
            self.arrived(((ring + 3) % 4, pair), q)
            (ring, pair), q = self.DOWN[t - 2]
            self.arrived(((ring + 1) % 4, pair), q)

    def finish(self):
        for line in self.lines.values():
            for copy in line[-self.WINDOW:]:
                copy.wait_send()


def gather_kernel(left, right, left_slots, right_slots, left_all, right_all, left_ids, right_ids,
                  ids, slots, left_send, left_recv, right_send, right_recv, sib_send, sib_recv,
                  idl_send, idl_recv, idr_send, idr_recv, own_sem):
    row, col = lax.axis_index("row"), lax.axis_index("col")
    y_hi, z = row // 4, lax.rem(row, 4)
    core, x, y_lo = lax.rem(col, 2), lax.rem(col // 2, 4), col // 8

    def left_place(ring, pair):
        return (lax.rem(y_lo + pair, 2) * 4 + lax.rem(x + ring, 4)) * 2 + core

    def right_place(ring, pair):
        return lax.rem(y_hi + pair, 2) * 4 + lax.rem(z + ring, 4)

    other = (row, col + 1 - 2 * core)

    fetch = [
        pltpu.make_async_copy(left_slots, slots.at[pl.ds(0, 1)], own_sem.at[4]),
        pltpu.make_async_copy(right_slots, slots.at[pl.ds(1, 1)], own_sem.at[5]),
    ]
    for copy in fetch:
        copy.start()
    barrier = pltpu.get_barrier_semaphore()
    for step in range(1, N_COL):
        pl.semaphore_signal(barrier, inc=1, device_id=(row, lax.rem(col + step, N_COL)), device_id_type=MESH)
    for step in range(1, N_ROW):
        pl.semaphore_signal(barrier, inc=1, device_id=(lax.rem(row + step, N_ROW), col), device_id_type=MESH)

    lane = lax.broadcasted_iota(jnp.int32, (1, LANES), 1)
    for copy in fetch:
        copy.wait()
    row_ids = jnp.full((1, LANES), -1, jnp.int32)
    for s in range(CAP):
        row_ids = jnp.where(lane == s, slots[0, s], row_ids)
        row_ids = jnp.where(lane == CAP + s, slots[1, s], row_ids)
    ids[...] = row_ids

    pl.semaphore_wait(barrier, N_COL + N_ROW - 2)

    shared = []

    def to_sibling(factor, slab, q):
        index = (slab[0] + 4 * slab[1]) * 4 + q
        part = factor.tile(slab, q)
        copy = pltpu.make_async_remote_copy(
            src_ref=factor.own.at[pl.ds(q * TILE, TILE)] if slab == (0, 0) else part,
            dst_ref=part,
            send_sem=sib_send.at[index],
            recv_sem=sib_recv.at[index],
            device_id=other,
            device_id_type=MESH,
        )
        copy.start()
        shared.append(copy)

    lf = Factor(left_all, left, left_place, lambda ring, pair: (row, left_place(ring, pair)), left_send, left_recv, to_sibling)
    rf = Factor(right_all, right, right_place, lambda ring, pair: (right_place(ring, pair), col), right_send, right_recv, None)

    lf.tick(0)
    rf.tick(0)
    lf.tick(1)
    rf.tick(1)

    small = []
    for step in range(1, N_COL):
        copy = pltpu.make_async_remote_copy(
            src_ref=ids, dst_ref=left_ids.at[col], send_sem=idl_send.at[step], recv_sem=idl_recv.at[step],
            device_id=(row, lax.rem(col + step, N_COL)), device_id_type=MESH)
        copy.start()
        small.append(copy)
    for step in range(1, N_ROW):
        copy = pltpu.make_async_remote_copy(
            src_ref=ids, dst_ref=right_ids.at[row], send_sem=idr_send.at[step], recv_sem=idr_recv.at[step],
            device_id=(lax.rem(row + step, N_ROW), col), device_id_type=MESH)
        copy.start()
        small.append(copy)
    for q in range(CAP):
        to_sibling(lf, (0, 0), q)
    local = [
        pltpu.make_async_copy(left, left_all.at[col], own_sem.at[0]),
        pltpu.make_async_copy(right, right_all.at[row], own_sem.at[1]),
        pltpu.make_async_copy(ids, left_ids.at[col], own_sem.at[2]),
        pltpu.make_async_copy(ids, right_ids.at[row], own_sem.at[3]),
    ]
    for copy in local:
        copy.start()

    for t in range(2, Factor.TICKS + 2):
        lf.tick(t)
        rf.tick(t)

    for copy in local:
        copy.wait()
    for index in range(8 * CAP):
        ring, pair, q = index // 4 % 4, index // 16, index % 4
        place = left_place(ring, pair) + 1 - 2 * core
        part = left_all.at[place, pl.ds(q * TILE, TILE)]
        pltpu.make_async_copy(part, part, sib_recv.at[index]).wait()
    for copy in small:
        copy.wait_recv()
    for copy in small + shared:
        copy.wait_send()
    lf.finish()
    rf.finish()


def gather(left, right, left_slots, right_slots):
    dma = pltpu.SemaphoreType.DMA
    operands = [pltpu.with_memory_space_constraint(x, pltpu.HBM) for x in (left, right, left_slots, right_slots)]
    return pl.pallas_call(
        gather_kernel,
        out_shape=[
            KEEP((N_COL, SLAB, TILE), jnp.bfloat16),
            KEEP((N_ROW, SLAB, TILE), jnp.bfloat16),
            jax.ShapeDtypeStruct((N_COL, 1, LANES), jnp.int32),
            jax.ShapeDtypeStruct((N_ROW, 1, LANES), jnp.int32),
        ],
        in_specs=[HBM, HBM, HBM, HBM],
        out_specs=[KEEP_SPEC, KEEP_SPEC, ANY, ANY],
        scratch_shapes=[
            pltpu.VMEM((1, LANES), jnp.int32),
            pltpu.SMEM((2, CAP), jnp.int32),
            dma((28,)), dma((32,)), dma((28,)), dma((32,)), dma((32,)), dma((32,)),
            dma((N_COL,)), dma((N_COL,)), dma((N_ROW,)), dma((N_ROW,)), dma((6,)),
        ],
        compiler_params=pltpu.CompilerParams(collective_id=0, has_side_effects=True, vmem_limit_bytes=2**20),
        name="gather_slabs",
    )(*operands)


def product_kernel(left_ids, right_ids, left_all, right_all, expanded, col_part):
    expanded[...] = jnp.zeros_like(expanded)

    def inner(n, _):
        q, s = n // CAP, lax.rem(n, CAP)
        held = right_ids[q, 0, CAP + s]

        @pl.when(held >= 0)
        def _():
            k, j = 2 * q + held // CB_DEV, lax.rem(held, CB_DEV)
            weights = right_all[q, pl.ds(pl.multiple_of(s * TILE, TILE), TILE)]
            part = jnp.dot(left_all[k], weights, preferred_element_type=jnp.float32)
            for u in range(CAP):
                i = left_ids[k, 0, u]
                i = jnp.where(i < 0, RB_DEV, i)
                at = (pl.ds(pl.multiple_of(i * TILE, TILE), TILE), pl.ds(pl.multiple_of(j * TILE, TILE), TILE))
                expanded[at] += part[u * TILE : (u + 1) * TILE]
        return 0

    lax.fori_loop(0, N_ROW * CAP, inner, 0)

    def add(i, total):
        part = expanded[pl.ds(pl.multiple_of(i * 64, 64), 64)]
        return total + jnp.sum((part * part).reshape(8, 8, CB_DEV * TILE), axis=0)

    total = lax.fori_loop(0, RB_DEV * TILE // 64, add, jnp.zeros((8, CB_DEV * TILE), jnp.float32))
    col_part[...] = jnp.sum(total, axis=0, keepdims=True)


def product(left_ids, right_ids, left_all, right_all):
    return pl.pallas_call(
        product_kernel,
        out_shape=[
            KEEP(((RB_DEV + 1) * TILE, CB_DEV * TILE), jnp.float32),
            jax.ShapeDtypeStruct((1, CB_DEV * TILE), jnp.float32),
        ],
        in_specs=[SMEM, SMEM, VMEM, VMEM],
        out_specs=[VMEM, VMEM],
        compiler_params=pltpu.CompilerParams(vmem_limit_bytes=4 * 2**20),
        name="tile_products",
    )(left_ids, right_ids, left_all, right_all)


def total_kernel(part, total, held, send, recv):
    row, col = lax.axis_index("row"), lax.axis_index("col")
    barrier = pltpu.get_barrier_semaphore()
    for step in range(1, N_ROW):
        pl.semaphore_signal(barrier, inc=1, device_id=(lax.rem(row + step, N_ROW), col), device_id_type=MESH)
    pl.semaphore_wait(barrier, N_ROW - 1)
    copies = []
    for step in range(1, N_ROW):
        copy = pltpu.make_async_remote_copy(
            src_ref=part, dst_ref=held.at[step], send_sem=send.at[step], recv_sem=recv.at[step],
            device_id=(lax.rem(row + step, N_ROW), col), device_id_type=MESH)
        copy.start()
        copies.append(copy)
    value = part[...]
    for step, copy in enumerate(copies):
        copy.wait_recv()
        value = value + held[step + 1]
    total[...] = value
    for copy in copies:
        copy.wait_send()


def column_total(part):
    dma = pltpu.SemaphoreType.DMA
    return pl.pallas_call(
        total_kernel,
        out_shape=jax.ShapeDtypeStruct(part.shape, part.dtype),
        in_specs=[VMEM],
        out_specs=VMEM,
        scratch_shapes=[pltpu.VMEM((N_ROW, *part.shape), part.dtype), dma((N_ROW,)), dma((N_ROW,))],
        compiler_params=pltpu.CompilerParams(collective_id=1, has_side_effects=True, vmem_limit_bytes=2**20),
        name="column_total",
    )(part)


SCALE_ROWS = 128
SCALE_SLOTS = 4


def scale_kernel(total, expanded, out, scaled, sems):
    factor = 1.0 / (total[...] / (RB_DEV * TILE * N_ROW) + EPSILON)
    copies = []
    for n in range(RB_DEV * TILE // SCALE_ROWS):
        slot = n % SCALE_SLOTS
        if n >= SCALE_SLOTS:
            copies[n - SCALE_SLOTS].wait()
        rows = pl.ds(n * SCALE_ROWS, SCALE_ROWS)
        value = expanded[rows]
        scaled[slot] = value * value * factor
        copy = pltpu.make_async_copy(scaled.at[slot], out.at[rows], sems.at[slot])
        copy.start()
        copies.append(copy)
    for copy in copies[-SCALE_SLOTS:]:
        copy.wait()


def scale(total, expanded):
    cols = expanded.shape[1]
    return pl.pallas_call(
        scale_kernel,
        out_shape=jax.ShapeDtypeStruct((RB_DEV * TILE, cols), jnp.float32),
        in_specs=[VMEM, VMEM],
        out_specs=ANY,
        scratch_shapes=[pltpu.VMEM((SCALE_SLOTS, SCALE_ROWS, cols), jnp.float32), pltpu.SemaphoreType.DMA((SCALE_SLOTS,))],
        compiler_params=pltpu.CompilerParams(vmem_limit_bytes=4 * 2**20),
        name="scale_columns",
    )(total, expanded)


KEEP = jax.ShapeDtypeStruct
KEEP_SPEC = ANY


def body(left_tiles, left_slots, right_tiles, right_slots):
    left = left_tiles.reshape(SLAB, TILE)
    right = right_tiles.reshape(SLAB, TILE)
    left_all, right_all, left_ids, right_ids = gather(
        left, right, left_slots.reshape(1, CAP), right_slots.reshape(1, CAP)
    )
    expanded, col_part = product(left_ids, right_ids, left_all, right_all)
    return scale(column_total(col_part), expanded)


def solution(mesh):
    placed = (P("row", "col", None), P("row", "col"), P("row", "col", None), P("row", "col"))
    return jax.shard_map(
        body, mesh=mesh, in_specs=placed, out_specs=P("row", "col"), check_vma=False
    )
```

time: 102 us -> 71.9 us (0.70)
  Pallas kernels: 88 us -> 70.9 us
  local copies, waits for them, and re-layouts: 13.4 us -> 0 us
    unnamed x14 -> x0, local copies, waits for them, and re-layouts: 13.4 us -> none
    pallas_call x2, Pallas kernels: 27.5 us -> 15.7 us  [the longest x1 11.8 us: product(): pl.pallas_call(product_kernel, out_shape=[KEEP(((RB_DEV + 1) * TILE, CB_D...]
    pallas_call x1, Pallas kernels: 10.7 us -> 7.88 us  [column_total(): pl.pallas_call(total_kernel, out_shape=jax.ShapeDtypeStruct(part.shape, p...]
    pallas_call x1, Pallas kernels: 49.8 us -> 47.3 us  [gather(): pl.pallas_call(gather_kernel, out_shape=[KEEP((N_COL, SLAB, TILE), jnp.bf...]
where the time goes in v2:
time: 71.9 us; the launch traced here: 70.9 us
  Pallas kernels  70.9 us (99%)
    pallas_call x1, Pallas kernels, gather(): pl.pallas_call(gather_kernel, out_shape=[KEEP((N_COL, SLAB, TILE), jnp.bf...  47.3 us
    pallas_call x1, Pallas kernels, product(): pl.pallas_call(product_kernel, out_shape=[KEEP(((RB_DEV + 1) * TILE, CB_D...  11.8 us
    pallas_call x1, Pallas kernels, column_total(): pl.pallas_call(total_kernel, out_shape=jax.ShapeDtypeStruct(part.shape, p...  7.88 us
    pallas_call x1, Pallas kernels, scale(): pl.pallas_call(scale_kernel, out_shape=jax.ShapeDtypeStruct((RB_DEV * TIL...  3.89 us

profile of v2, /device:TPU:0, one launch (start us, length us, event | category | flops | bytes accessed | tf_op | source)
XLA Modules:
  0.0 70.9 jit_solution(10630902580161663041)
XLA Ops:
  0.0 47.3 %gather_slabs.1 = (bf16[16,1024,256]{2,1,0:T(8,128)(2,1)S(1)}, bf16[8,1024,256]{2,1,0:T(8,128)(2,1)S(1)}, s32[16,1,128]{2,1,0:T(1,128)S(1)}, s32[8,1,128]{2,1,0:T(1,128)S(1)}) custom-call(bf16[1024,256]{1,0:T(8,128)(2,1)} %bitcast.4, bf16[1024,256]{1,0:T(8,128)(2,1)} %bitcast.5, s32[1,4]{1,0:T(1,128)} %bitcast.6, s32[1,4]{1,0:T(1,128)} %bitcast.7), custom_call_target="tpu_custom_call" | custom-call | tf_op jit(solution)/shard_map/gather_slabs/pallas_call | solution.py:196
  47.4 11.8 %tile_products.1 = (f32[2304,1024]{1,0:T(8,128)S(1)}, f32[1,1024]{1,0:T(1,128)S(1)}) custom-call(s32[16,1,128]{2,1,0:T(1,128)S(1)} %get-tuple-element.11.left_ids, s32[8,1,128]{2,1,0:T(1,128)S(1)} %get-tuple-element.12.right_ids, bf16[16,1024,256]{2,1,0:T(8,128)(2,1)S(1)} %get-tuple-element.13.left_all, bf16[8,1024,256]{2,1,0:T(8,128)(2,1)S(1)} %get-tuple-element.14.right_all), custom_call_target="tpu_custom_call" | custom-call | tf_op jit(solution)/shard_map/tile_products/pallas_call | solution.py:247
  59.1 7.9 %column_total.1.total = f32[1,1024]{1,0:T(1,128)S(1)} custom-call(f32[1,1024]{1,0:T(1,128)S(1)} %get-tuple-element.15.part), custom_call_target="tpu_custom_call" | custom-call | tf_op jit(solution)/shard_map/column_total/pallas_call | solution.py:284
  67.0 3.9 %scale_columns.1 = f32[2048,1024]{1,0:T(8,128)} custom-call(f32[1,1024]{1,0:T(1,128)S(1)} %column_total.1.total, f32[2304,1024]{1,0:T(8,128)S(1)} %get-tuple-element.16.expanded), custom_call_target="tpu_custom_call" | custom-call | tf_op jit(solution)/shard_map/scale_columns/pallas_call | solution.py:318

commit v3 on v2

--- a/solution.py
+++ b/solution.py
@@ -20,7 +20,9 @@
 ANY = pl.BlockSpec(memory_space=pl.ANY)
 VMEM = pl.BlockSpec(memory_space=pltpu.VMEM)
 SMEM = pl.BlockSpec(memory_space=pltpu.SMEM)
-HBM = pl.BlockSpec(memory_space=pltpu.HBM)
+
+
+IDS_ALONG = [("pair", (0, 0)), ("up", (0, 0)), ("up", (3, 0)), ("up", (0, 1)), ("up", (3, 1)), ("down", (0, 0)), ("down", (0, 1))]
 
 
 class Factor:
@@ -29,10 +31,12 @@
     TICKS = len(UP)
     WINDOW = 2
 
-    def __init__(self, out, own, place, device, send, recv, sibling):
+    def __init__(self, out, own, place, device, send, recv, sibling, ids_out, ids_own, ids_place, ids_send, ids_recv):
         self.out, self.own, self.place, self.device = out, own, place, device
         self.send, self.recv, self.sibling = send, recv, sibling
-        self.count, self.here = 0, set()
+        self.ids_out, self.ids_own, self.ids_place, self.ids_send, self.ids_recv = ids_out, ids_own, ids_place, ids_send, ids_recv
+        self.count, self.here, self.ids_here, self.ids_sent = 0, set(), set(), []
+        self.lines_with_ids = {(line, slab) for line, slab in IDS_ALONG}
         self.lines = {"up": [], "down": [], "pair": []}
 
     def tile(self, slab, q):
@@ -57,6 +61,29 @@
         copy.start()
         self.count += 1
         sent.append(copy)
+        if (line, slab) in self.lines_with_ids:
+            self.lines_with_ids.remove((line, slab))
+            self.start_ids(slab, there, ring, pair)
+
+    def start_ids(self, slab, there, ring, pair):
+        if slab != (0, 0):
+            self.ids_arrived(slab)
+        copy = pltpu.make_async_remote_copy(
+            src_ref=self.ids_own if slab == (0, 0) else self.ids_out.at[self.ids_place(*slab)],
+            dst_ref=self.ids_out.at[self.ids_place(*slab)],
+            send_sem=self.ids_send.at[len(self.ids_sent)],
+            recv_sem=self.ids_recv.at[there[0] + 4 * there[1]],
+            device_id=self.device(ring, pair),
+            device_id_type=MESH,
+        )
+        copy.start()
+        self.ids_sent.append(copy)
+
+    def ids_arrived(self, slab):
+        if slab not in self.ids_here:
+            self.ids_here.add(slab)
+            here = self.ids_out.at[self.ids_place(*slab)]
+            pltpu.make_async_copy(here, here, self.ids_recv.at[slab[0] + 4 * slab[1]]).wait()
 
     def arrived(self, slab, q):
         if (slab, q) in self.here:
@@ -83,11 +110,13 @@
         for line in self.lines.values():
             for copy in line[-self.WINDOW:]:
                 copy.wait_send()
+        for copy in self.ids_sent:
+            copy.wait_send()
 
 
 def gather_kernel(left, right, left_slots, right_slots, left_all, right_all, left_ids, right_ids,
                   ids, slots, left_send, left_recv, right_send, right_recv, sib_send, sib_recv,
-                  idl_send, idl_recv, idr_send, idr_recv, own_sem):
+                  idl_send, idl_recv, idr_send, idr_recv, ids_sib, own_sem):
     row, col = lax.axis_index("row"), lax.axis_index("col")
     y_hi, z = row // 4, lax.rem(row, 4)
     core, x, y_lo = lax.rem(col, 2), lax.rem(col // 2, 4), col // 8
@@ -107,10 +136,11 @@
     for copy in fetch:
         copy.start()
     barrier = pltpu.get_barrier_semaphore()
-    for step in range(1, N_COL):
-        pl.semaphore_signal(barrier, inc=1, device_id=(row, lax.rem(col + step, N_COL)), device_id_type=MESH)
-    for step in range(1, N_ROW):
-        pl.semaphore_signal(barrier, inc=1, device_id=(lax.rem(row + step, N_ROW), col), device_id_type=MESH)
+    for peer in (
+        (row, left_place(1, 0)), (row, left_place(3, 0)), (row, left_place(0, 1)), other,
+        (right_place(1, 0), col), (right_place(3, 0), col), (right_place(0, 1), col),
+    ):
+        pl.semaphore_signal(barrier, inc=1, device_id=peer, device_id_type=MESH)
 
     lane = lax.broadcasted_iota(jnp.int32, (1, LANES), 1)
     for copy in fetch:
@@ -121,7 +151,7 @@
         row_ids = jnp.where(lane == CAP + s, slots[1, s], row_ids)
     ids[...] = row_ids
 
-    pl.semaphore_wait(barrier, N_COL + N_ROW - 2)
+    pl.semaphore_wait(barrier, 7)
 
     shared = []
 
@@ -139,33 +169,29 @@
         copy.start()
         shared.append(copy)
 
-    lf = Factor(left_all, left, left_place, lambda ring, pair: (row, left_place(ring, pair)), left_send, left_recv, to_sibling)
-    rf = Factor(right_all, right, right_place, lambda ring, pair: (right_place(ring, pair), col), right_send, right_recv, None)
+    def left_ids_place(ring, pair):
+        return core * N_ROW + left_place(ring, pair) // 2
+
+    lf = Factor(
+        left_all, left, left_place, lambda ring, pair: (row, left_place(ring, pair)), left_send, left_recv, to_sibling,
+        left_ids, ids, left_ids_place, idl_send, idl_recv,
+    )
+    rf = Factor(
+        right_all, right, right_place, lambda ring, pair: (right_place(ring, pair), col), right_send, right_recv, None,
+        right_ids, ids, right_place, idr_send, idr_recv,
+    )
 
     lf.tick(0)
     rf.tick(0)
     lf.tick(1)
     rf.tick(1)
 
-    small = []
-    for step in range(1, N_COL):
-        copy = pltpu.make_async_remote_copy(
-            src_ref=ids, dst_ref=left_ids.at[col], send_sem=idl_send.at[step], recv_sem=idl_recv.at[step],
-            device_id=(row, lax.rem(col + step, N_COL)), device_id_type=MESH)
-        copy.start()
-        small.append(copy)
-    for step in range(1, N_ROW):
-        copy = pltpu.make_async_remote_copy(
-            src_ref=ids, dst_ref=right_ids.at[row], send_sem=idr_send.at[step], recv_sem=idr_recv.at[step],
-            device_id=(lax.rem(row + step, N_ROW), col), device_id_type=MESH)
-        copy.start()
-        small.append(copy)
     for q in range(CAP):
         to_sibling(lf, (0, 0), q)
     local = [
         pltpu.make_async_copy(left, left_all.at[col], own_sem.at[0]),
         pltpu.make_async_copy(right, right_all.at[row], own_sem.at[1]),
-        pltpu.make_async_copy(ids, left_ids.at[col], own_sem.at[2]),
+        pltpu.make_async_copy(ids, left_ids.at[left_ids_place(0, 0)], own_sem.at[2]),
         pltpu.make_async_copy(ids, right_ids.at[row], own_sem.at[3]),
     ]
     for copy in local:
@@ -177,14 +203,22 @@
 
     for copy in local:
         copy.wait()
+    for slab in [(ring, pair) for pair in range(2) for ring in range(4)][1:]:
+        lf.ids_arrived(slab)
+        rf.ids_arrived(slab)
+    block = left_ids.at[pl.ds(core * N_ROW, N_ROW)]
+    copy = pltpu.make_async_remote_copy(
+        src_ref=block, dst_ref=block, send_sem=ids_sib.at[0], recv_sem=ids_sib.at[1], device_id=other, device_id_type=MESH)
+    copy.start()
+    shared.append(copy)
     for index in range(8 * CAP):
         ring, pair, q = index // 4 % 4, index // 16, index % 4
         place = left_place(ring, pair) + 1 - 2 * core
         part = left_all.at[place, pl.ds(q * TILE, TILE)]
         pltpu.make_async_copy(part, part, sib_recv.at[index]).wait()
-    for copy in small:
-        copy.wait_recv()
-    for copy in small + shared:
+    theirs = left_ids.at[pl.ds((1 - core) * N_ROW, N_ROW)]
+    pltpu.make_async_copy(theirs, theirs, ids_sib.at[1]).wait()
+    for copy in shared:
         copy.wait_send()
     lf.finish()
     rf.finish()
@@ -196,100 +230,110 @@
     return pl.pallas_call(
         gather_kernel,
         out_shape=[
-            KEEP((N_COL, SLAB, TILE), jnp.bfloat16),
-            KEEP((N_ROW, SLAB, TILE), jnp.bfloat16),
+            jax.ShapeDtypeStruct((N_COL, SLAB, TILE), jnp.bfloat16),
+            jax.ShapeDtypeStruct((N_ROW, SLAB, TILE), jnp.bfloat16),
             jax.ShapeDtypeStruct((N_COL, 1, LANES), jnp.int32),
             jax.ShapeDtypeStruct((N_ROW, 1, LANES), jnp.int32),
         ],
-        in_specs=[HBM, HBM, HBM, HBM],
-        out_specs=[KEEP_SPEC, KEEP_SPEC, ANY, ANY],
+        in_specs=[ANY, ANY, ANY, ANY],
+        out_specs=[ANY, ANY, ANY, ANY],
         scratch_shapes=[
             pltpu.VMEM((1, LANES), jnp.int32),
             pltpu.SMEM((2, CAP), jnp.int32),
             dma((28,)), dma((32,)), dma((28,)), dma((32,)), dma((32,)), dma((32,)),
-            dma((N_COL,)), dma((N_COL,)), dma((N_ROW,)), dma((N_ROW,)), dma((6,)),
+            dma((7,)), dma((8,)), dma((7,)), dma((8,)), dma((2,)), dma((6,)),
         ],
         compiler_params=pltpu.CompilerParams(collective_id=0, has_side_effects=True, vmem_limit_bytes=2**20),
         name="gather_slabs",
     )(*operands)
 
 
-def product_kernel(left_ids, right_ids, left_all, right_all, expanded, col_part):
+PER_STEP = 8
+
+
+def product_kernel(left_ids, right_ids, left_all, right_all, expanded):
     expanded[...] = jnp.zeros_like(expanded)
 
     def inner(n, _):
-        q, s = n // CAP, lax.rem(n, CAP)
-        held = right_ids[q, 0, CAP + s]
-
-        @pl.when(held >= 0)
-        def _():
-            k, j = 2 * q + held // CB_DEV, lax.rem(held, CB_DEV)
-            weights = right_all[q, pl.ds(pl.multiple_of(s * TILE, TILE), TILE)]
-            part = jnp.dot(left_all[k], weights, preferred_element_type=jnp.float32)
+        work = []
+        for w in range(PER_STEP):
+            q, s = n * (PER_STEP // CAP) + w // CAP, w % CAP
+            held = right_ids[q, 0, CAP + s]
+            kept = held >= 0
+            held = jnp.where(kept, held, 0)
+            parity = held // CB_DEV
+            rows = []
             for u in range(CAP):
-                i = left_ids[k, 0, u]
-                i = jnp.where(i < 0, RB_DEV, i)
+                i = left_ids[parity * N_ROW + q, 0, u]
+                rows.append(jnp.where(kept & (i >= 0), i, RB_DEV))
+            work.append((q, s, 2 * q + parity, lax.rem(held, CB_DEV), rows))
+        for q, s, k, j, rows in work:
+            weights = right_all[q, s * TILE : (s + 1) * TILE]
+            for u, i in enumerate(rows):
                 at = (pl.ds(pl.multiple_of(i * TILE, TILE), TILE), pl.ds(pl.multiple_of(j * TILE, TILE), TILE))
-                expanded[at] += part[u * TILE : (u + 1) * TILE]
+                expanded[at] += jnp.dot(
+                    left_all[k, u * TILE : (u + 1) * TILE], weights, preferred_element_type=jnp.float32
+                )
         return 0
 
-    lax.fori_loop(0, N_ROW * CAP, inner, 0)
-
-    def add(i, total):
-        part = expanded[pl.ds(pl.multiple_of(i * 64, 64), 64)]
-        return total + jnp.sum((part * part).reshape(8, 8, CB_DEV * TILE), axis=0)
-
-    total = lax.fori_loop(0, RB_DEV * TILE // 64, add, jnp.zeros((8, CB_DEV * TILE), jnp.float32))
-    col_part[...] = jnp.sum(total, axis=0, keepdims=True)
+    lax.fori_loop(0, N_ROW * CAP // PER_STEP, inner, 0)
 
 
 def product(left_ids, right_ids, left_all, right_all):
     return pl.pallas_call(
         product_kernel,
-        out_shape=[
-            KEEP(((RB_DEV + 1) * TILE, CB_DEV * TILE), jnp.float32),
-            jax.ShapeDtypeStruct((1, CB_DEV * TILE), jnp.float32),
-        ],
+        out_shape=jax.ShapeDtypeStruct(((RB_DEV + 1) * TILE, CB_DEV * TILE), jnp.float32),
         in_specs=[SMEM, SMEM, VMEM, VMEM],
-        out_specs=[VMEM, VMEM],
+        out_specs=VMEM,
         compiler_params=pltpu.CompilerParams(vmem_limit_bytes=4 * 2**20),
         name="tile_products",
     )(left_ids, right_ids, left_all, right_all)
 
 
-def total_kernel(part, total, held, send, recv):
+def total_kernel(expanded, total, part, held, send, recv):
     row, col = lax.axis_index("row"), lax.axis_index("col")
+    peers = [(lax.rem(row + step, N_ROW), col) for step in range(1, N_ROW)]
     barrier = pltpu.get_barrier_semaphore()
-    for step in range(1, N_ROW):
-        pl.semaphore_signal(barrier, inc=1, device_id=(lax.rem(row + step, N_ROW), col), device_id_type=MESH)
+    for peer in peers:
+        pl.semaphore_signal(barrier, inc=1, device_id=peer, device_id_type=MESH)
+
+    def add(i, sums):
+        rows = expanded[pl.ds(pl.multiple_of(i * 64, 64), 64)]
+        return sums + jnp.sum((rows * rows).reshape(8, 8, CB_DEV * TILE), axis=0)
+
+    sums = lax.fori_loop(0, RB_DEV * TILE // 64, add, jnp.zeros((8, CB_DEV * TILE), jnp.float32))
+    part[...] = jnp.sum(sums, axis=0, keepdims=True)
     pl.semaphore_wait(barrier, N_ROW - 1)
     copies = []
-    for step in range(1, N_ROW):
+    for n, peer in enumerate(peers):
         copy = pltpu.make_async_remote_copy(
-            src_ref=part, dst_ref=held.at[step], send_sem=send.at[step], recv_sem=recv.at[step],
-            device_id=(lax.rem(row + step, N_ROW), col), device_id_type=MESH)
+            src_ref=part, dst_ref=held.at[n], send_sem=send.at[n], recv_sem=recv.at[n],
+            device_id=peer, device_id_type=MESH)
         copy.start()
         copies.append(copy)
     value = part[...]
-    for step, copy in enumerate(copies):
+    for n, copy in enumerate(copies):
         copy.wait_recv()
-        value = value + held[step + 1]
+        value = value + held[n]
     total[...] = value
     for copy in copies:
         copy.wait_send()
 
 
-def column_total(part):
+def column_total(expanded):
     dma = pltpu.SemaphoreType.DMA
+    shape = (1, CB_DEV * TILE)
     return pl.pallas_call(
         total_kernel,
-        out_shape=jax.ShapeDtypeStruct(part.shape, part.dtype),
+        out_shape=jax.ShapeDtypeStruct(shape, jnp.float32),
         in_specs=[VMEM],
         out_specs=VMEM,
-        scratch_shapes=[pltpu.VMEM((N_ROW, *part.shape), part.dtype), dma((N_ROW,)), dma((N_ROW,))],
+        scratch_shapes=[
+            pltpu.VMEM(shape, jnp.float32), pltpu.VMEM((N_ROW - 1, *shape), jnp.float32), dma((N_ROW - 1,)), dma((N_ROW - 1,)),
+        ],
         compiler_params=pltpu.CompilerParams(collective_id=1, has_side_effects=True, vmem_limit_bytes=2**20),
         name="column_total",
-    )(part)
+    )(expanded)
 
 
 SCALE_ROWS = 128
@@ -326,18 +370,14 @@
     )(total, expanded)
 
 
-KEEP = jax.ShapeDtypeStruct
-KEEP_SPEC = ANY
-
-
 def body(left_tiles, left_slots, right_tiles, right_slots):
     left = left_tiles.reshape(SLAB, TILE)
     right = right_tiles.reshape(SLAB, TILE)
     left_all, right_all, left_ids, right_ids = gather(
         left, right, left_slots.reshape(1, CAP), right_slots.reshape(1, CAP)
     )
-    expanded, col_part = product(left_ids, right_ids, left_all, right_all)
-    return scale(column_total(col_part), expanded)
+    expanded = product(left_ids, right_ids, left_all, right_all)
+    return scale(column_total(expanded), expanded)
 
 
 def solution(mesh):

time: 71.9 us -> 66.8 us (0.929)
  Pallas kernels: 70.9 us -> 66.5 us
    pallas_call x3, Pallas kernels: 67 us -> 62.6 us  [the longest x1 46 us: gather(): pl.pallas_call(gather_kernel, out_shape=[jax.ShapeDtypeStruct((N_COL, SLA...]
where the time goes in v3:
time: 66.8 us; the launch traced here: 66.5 us
  Pallas kernels  66.5 us (100%)
    pallas_call x1, Pallas kernels, gather(): pl.pallas_call(gather_kernel, out_shape=[jax.ShapeDtypeStruct((N_COL, SLA...  46 us
    pallas_call x1, Pallas kernels, product(): pl.pallas_call(product_kernel, out_shape=jax.ShapeDtypeStruct(((RB_DEV +...  8.8 us
    pallas_call x1, Pallas kernels, column_total(): pl.pallas_call(total_kernel, out_shape=jax.ShapeDtypeStruct(shape, jnp.fl...  7.79 us
    pallas_call x1, Pallas kernels, scale(): pl.pallas_call(scale_kernel, out_shape=jax.ShapeDtypeStruct((RB_DEV * TIL...  3.89 us

profile of v3, /device:TPU:0, one launch (start us, length us, event | category | flops | bytes accessed | tf_op | source)
XLA Modules:
  0.0 66.5 jit_solution(830292884935400549)
XLA Ops:
  0.0 46.0 %gather_slabs.1 = (bf16[16,1024,256]{2,1,0:T(8,128)(2,1)S(1)}, bf16[8,1024,256]{2,1,0:T(8,128)(2,1)S(1)}, s32[16,1,128]{2,1,0:T(1,128)S(1)}, s32[8,1,128]{2,1,0:T(1,128)S(1)}) custom-call(bf16[1024,256]{1,0:T(8,128)(2,1)} %bitcast.4, bf16[1024,256]{1,0:T(8,128)(2,1)} %bitcast.5, s32[1,4]{1,0:T(1,128)} %bitcast.6, s32[1,4]{1,0:T(1,128)} %bitcast.7), custom_call_target="tpu_custom_call" | custom-call | tf_op jit(solution)/shard_map/gather_slabs/pallas_call | solution.py:230
  46.0 8.8 %tile_products.1.expanded = f32[2304,1024]{1,0:T(8,128)S(1)} custom-call(s32[16,1,128]{2,1,0:T(1,128)S(1)} %get-tuple-element.9.left_ids, s32[8,1,128]{2,1,0:T(1,128)S(1)} %get-tuple-element.10.right_ids, bf16[16,1024,256]{2,1,0:T(8,128)(2,1)S(1)} %get-tuple-element.11.left_all, bf16[8,1024,256]{2,1,0:T(8,128)(2,1)S(1)} %get-tuple-element.12.right_all), custom_call_target="tpu_custom_call" | custom-call | tf_op jit(solution)/shard_map/tile_products/pallas_call | solution.py:283
  54.8 7.8 %column_total.1.total = f32[1,1024]{1,0:T(1,128)S(1)} custom-call(f32[2304,1024]{1,0:T(8,128)S(1)} %tile_products.1.expanded), custom_call_target="tpu_custom_call" | custom-call | tf_op jit(solution)/shard_map/column_total/pallas_call | solution.py:326
  62.6 3.9 %scale_columns.1 = f32[2048,1024]{1,0:T(8,128)} custom-call(f32[1,1024]{1,0:T(1,128)S(1)} %column_total.1.total, f32[2304,1024]{1,0:T(8,128)S(1)} %tile_products.1.expanded), custom_call_target="tpu_custom_call" | custom-call | tf_op jit(solution)/shard_map/scale_columns/pallas_call | solution.py:362

commit v4 on v3

--- a/solution.py
+++ b/solution.py
@@ -22,16 +22,24 @@
 SMEM = pl.BlockSpec(memory_space=pltpu.SMEM)
 
 
-IDS_ALONG = [("pair", (0, 0)), ("up", (0, 0)), ("up", (3, 0)), ("up", (0, 1)), ("up", (3, 1)), ("down", (0, 0)), ("down", (0, 1))]
+IDS_ALONG = [("pair", (0, 0)), ("up", (0, 0)), ("up", (3, 0)), ("up", (0, 1)), ("down", (0, 0)), ("down", (0, 1))]
+PIECES = [(0, TILE), (TILE, TILE), (2 * TILE, TILE), (3 * TILE, TILE), (2 * TILE, TILE // 2), (2 * TILE + TILE // 2, TILE // 2)]
 
 
 class Factor:
-    UP = [((0, 0), q) for q in (0, 1, 2, 3)] + [((3, 0), 0), ((3, 0), 2)] + [((0, 1), q) for q in (0, 1, 2, 3)] + [((3, 1), 0), ((3, 1), 2)]
-    DOWN = [((0, 0), q) for q in (1, 0, 3, 2)] + [((1, 0), 1), ((1, 0), 3)] + [((0, 1), q) for q in (1, 0, 2, 3)] + [((1, 1), 1), ((1, 1), 3)]
-    TICKS = len(UP)
     WINDOW = 2
 
-    def __init__(self, out, own, place, device, send, recv, sibling, ids_out, ids_own, ids_place, ids_send, ids_recv):
+    def __init__(self, out, own, place, device, send, recv, sibling, ids_out, ids_own, ids_place, ids_send, ids_recv, across):
+        self.across = across
+        halves = 2 not in across
+        self.UP = [((0, 0), q) for q in (0, 1, 2, 3)] + [((3, 0), 0), ((3, 0), 2)] + [((0, 1), q) for q in (0, 1, 2, 3)] + [((3, 1), 0)]
+        self.DOWN = [((0, 0), q) for q in (1, 0, 3, 2)] + [((1, 0), 1), ((1, 0), 3)] + [((0, 1), q) for q in (1, 0, 2, 3)] + [((1, 1), 1)]
+        if halves:
+            self.UP.append(((3, 1), 4))
+            self.DOWN.append(((1, 1), 5))
+        self.PAIR = {0: ((0, 0), 0), 2: ((0, 0), 1), 4: ((0, 0), 2), 6: ((0, 0), 3)}
+        for n, q in enumerate(across):
+            self.PAIR[8 + n] = ((2, 0), q)
         self.out, self.own, self.place, self.device = out, own, place, device
         self.send, self.recv, self.sibling = send, recv, sibling
         self.ids_out, self.ids_own, self.ids_place, self.ids_send, self.ids_recv = ids_out, ids_own, ids_place, ids_send, ids_recv
@@ -40,21 +48,21 @@
         self.lines = {"up": [], "down": [], "pair": []}
 
     def tile(self, slab, q):
-        return self.out.at[self.place(*slab), pl.ds(q * TILE, TILE)]
+        return self.out.at[self.place(*slab), pl.ds(*PIECES[q])]
 
     def start(self, line, slab, q, ring, pair):
         sent = self.lines[line]
         if len(sent) >= self.WINDOW:
             sent[-self.WINDOW].wait_send()
         if slab != (0, 0):
-            self.arrived(slab, q)
+            self.arrived(slab, min(q, 2) if q > 3 else q)
         there = ((slab[0] - ring) % 4, (slab[1] - pair) % 2)
-        source = self.own.at[pl.ds(q * TILE, TILE)] if slab == (0, 0) else self.tile(slab, q)
+        source = self.own.at[pl.ds(*PIECES[q])] if slab == (0, 0) else self.tile(slab, q)
         copy = pltpu.make_async_remote_copy(
             src_ref=source,
             dst_ref=self.tile(slab, q),
             send_sem=self.send.at[self.count],
-            recv_sem=self.recv.at[(there[0] + 4 * there[1]) * 4 + q],
+            recv_sem=self.recv.at[(there[0] + 4 * there[1]) * len(PIECES) + q],
             device_id=self.device(ring, pair),
             device_id_type=MESH,
         )
@@ -90,21 +98,26 @@
             return
         self.here.add((slab, q))
         here = self.tile(slab, q)
-        pltpu.make_async_copy(here, here, self.recv.at[(slab[0] + 4 * slab[1]) * 4 + q]).wait()
+        pltpu.make_async_copy(here, here, self.recv.at[(slab[0] + 4 * slab[1]) * len(PIECES) + q]).wait()
         if self.sibling is not None:
             self.sibling(self, slab, q)
 
     def tick(self, t):
-        if t % 2 == 0 and t // 2 < CAP:
-            self.start("pair", (0, 0), t // 2, 0, 1)
-        if t < self.TICKS:
+        if t in self.PAIR:
+            self.start("pair", *self.PAIR[t], 0, 1)
+        if t < len(self.UP):
             self.start("up", *self.UP[t], 1, 0)
             self.start("down", *self.DOWN[t], 3, 0)
-        if 2 <= t < self.TICKS + 2:
+        if t == 8:
+            self.start_ids((3, 1), (2, 1), 1, 0)
+        if 2 <= t < len(self.UP) + 2:
             (ring, pair), q = self.UP[t - 2]
             self.arrived(((ring + 3) % 4, pair), q)
             (ring, pair), q = self.DOWN[t - 2]
             self.arrived(((ring + 1) % 4, pair), q)
+        if t - 3 in self.PAIR:
+            slab, q = self.PAIR[t - 3]
+            self.arrived((slab[0], 1), q)
 
     def finish(self):
         for line in self.lines.values():
@@ -174,11 +187,11 @@
 
     lf = Factor(
         left_all, left, left_place, lambda ring, pair: (row, left_place(ring, pair)), left_send, left_recv, to_sibling,
-        left_ids, ids, left_ids_place, idl_send, idl_recv,
+        left_ids, ids, left_ids_place, idl_send, idl_recv, (2, 3),
     )
     rf = Factor(
         right_all, right, right_place, lambda ring, pair: (right_place(ring, pair), col), right_send, right_recv, None,
-        right_ids, ids, right_place, idr_send, idr_recv,
+        right_ids, ids, right_place, idr_send, idr_recv, (3,),
     )
 
     lf.tick(0)
@@ -197,20 +210,23 @@
     for copy in local:
         copy.start()
 
-    for t in range(2, Factor.TICKS + 2):
+    slabs = [(ring, pair) for pair in range(2) for ring in range(4)][1:]
+    for t in range(2, 14):
         lf.tick(t)
+        if t == 12:
+            for copy in local:
+                copy.wait()
+            for slab in slabs:
+                lf.ids_arrived(slab)
+            block = left_ids.at[pl.ds(core * N_ROW, N_ROW)]
+            copy = pltpu.make_async_remote_copy(
+                src_ref=block, dst_ref=block, send_sem=ids_sib.at[0], recv_sem=ids_sib.at[1], device_id=other, device_id_type=MESH)
+            copy.start()
+            shared.append(copy)
         rf.tick(t)
-
-    for copy in local:
-        copy.wait()
-    for slab in [(ring, pair) for pair in range(2) for ring in range(4)][1:]:
-        lf.ids_arrived(slab)
+    for slab in slabs:
         rf.ids_arrived(slab)
-    block = left_ids.at[pl.ds(core * N_ROW, N_ROW)]
-    copy = pltpu.make_async_remote_copy(
-        src_ref=block, dst_ref=block, send_sem=ids_sib.at[0], recv_sem=ids_sib.at[1], device_id=other, device_id_type=MESH)
-    copy.start()
-    shared.append(copy)
+
     for index in range(8 * CAP):
         ring, pair, q = index // 4 % 4, index // 16, index % 4
         place = left_place(ring, pair) + 1 - 2 * core
@@ -240,7 +256,7 @@
         scratch_shapes=[
             pltpu.VMEM((1, LANES), jnp.int32),
             pltpu.SMEM((2, CAP), jnp.int32),
-            dma((28,)), dma((32,)), dma((28,)), dma((32,)), dma((32,)), dma((32,)),
+            dma((28,)), dma((48,)), dma((29,)), dma((48,)), dma((32,)), dma((32,)),
             dma((7,)), dma((8,)), dma((7,)), dma((8,)), dma((2,)), dma((6,)),
         ],
         compiler_params=pltpu.CompilerParams(collective_id=0, has_side_effects=True, vmem_limit_bytes=2**20),
@@ -249,6 +265,7 @@
 
 
 PER_STEP = 8
+HALF = TILE // 2
 
 
 def product_kernel(left_ids, right_ids, left_all, right_all, expanded):
@@ -270,10 +287,10 @@
         for q, s, k, j, rows in work:
             weights = right_all[q, s * TILE : (s + 1) * TILE]
             for u, i in enumerate(rows):
-                at = (pl.ds(pl.multiple_of(i * TILE, TILE), TILE), pl.ds(pl.multiple_of(j * TILE, TILE), TILE))
-                expanded[at] += jnp.dot(
-                    left_all[k, u * TILE : (u + 1) * TILE], weights, preferred_element_type=jnp.float32
-                )
+                for h in range(TILE // HALF):
+                    expanded[i * CB_DEV + j, h * HALF : (h + 1) * HALF] += jnp.dot(
+                        left_all[k, u * TILE + h * HALF : u * TILE + (h + 1) * HALF], weights, preferred_element_type=jnp.float32
+                    )
         return 0
 
     lax.fori_loop(0, N_ROW * CAP // PER_STEP, inner, 0)
@@ -282,7 +299,7 @@
 def product(left_ids, right_ids, left_all, right_all):
     return pl.pallas_call(
         product_kernel,
-        out_shape=jax.ShapeDtypeStruct(((RB_DEV + 1) * TILE, CB_DEV * TILE), jnp.float32),
+        out_shape=jax.ShapeDtypeStruct(((RB_DEV + 1) * CB_DEV, TILE, TILE), jnp.float32),
         in_specs=[SMEM, SMEM, VMEM, VMEM],
         out_specs=VMEM,
         compiler_params=pltpu.CompilerParams(vmem_limit_bytes=4 * 2**20),
@@ -297,12 +314,14 @@
     for peer in peers:
         pl.semaphore_signal(barrier, inc=1, device_id=peer, device_id_type=MESH)
 
-    def add(i, sums):
-        rows = expanded[pl.ds(pl.multiple_of(i * 64, 64), 64)]
-        return sums + jnp.sum((rows * rows).reshape(8, 8, CB_DEV * TILE), axis=0)
-
-    sums = lax.fori_loop(0, RB_DEV * TILE // 64, add, jnp.zeros((8, CB_DEV * TILE), jnp.float32))
-    part[...] = jnp.sum(sums, axis=0, keepdims=True)
+    for j in range(CB_DEV):
+
+        def add(i, sums):
+            rows = expanded[i * CB_DEV + j]
+            return sums + jnp.sum((rows * rows).reshape(TILE // 16, 16, TILE), axis=0)
+
+        sums = lax.fori_loop(0, RB_DEV, add, jnp.zeros((16, TILE), jnp.float32))
+        part[:, j * TILE : (j + 1) * TILE] = jnp.sum(sums, axis=0, keepdims=True)
     pl.semaphore_wait(barrier, N_ROW - 1)
     copies = []
     for n, peer in enumerate(peers):
@@ -347,10 +366,12 @@
         slot = n % SCALE_SLOTS
         if n >= SCALE_SLOTS:
             copies[n - SCALE_SLOTS].wait()
-        rows = pl.ds(n * SCALE_ROWS, SCALE_ROWS)
-        value = expanded[rows]
-        scaled[slot] = value * value * factor
-        copy = pltpu.make_async_copy(scaled.at[slot], out.at[rows], sems.at[slot])
+        i, first = n * SCALE_ROWS // TILE, n * SCALE_ROWS % TILE
+        for j in range(CB_DEV):
+            columns = slice(j * TILE, (j + 1) * TILE)
+            value = expanded[i * CB_DEV + j, first : first + SCALE_ROWS]
+            scaled[slot, :, columns] = value * value * factor[:, columns]
+        copy = pltpu.make_async_copy(scaled.at[slot], out.at[pl.ds(n * SCALE_ROWS, SCALE_ROWS)], sems.at[slot])
         copy.start()
         copies.append(copy)
     for copy in copies[-SCALE_SLOTS:]:
@@ -358,10 +379,10 @@
 
 
 def scale(total, expanded):
-    cols = expanded.shape[1]
+    rows, cols = RB_DEV * TILE, CB_DEV * TILE
     return pl.pallas_call(
         scale_kernel,
-        out_shape=jax.ShapeDtypeStruct((RB_DEV * TILE, cols), jnp.float32),
+        out_shape=jax.ShapeDtypeStruct((rows, cols), jnp.float32),
         in_specs=[VMEM, VMEM],
         out_specs=ANY,
         scratch_shapes=[pltpu.VMEM((SCALE_SLOTS, SCALE_ROWS, cols), jnp.float32), pltpu.SemaphoreType.DMA((SCALE_SLOTS,))],

time: 66.8 us -> 63.2 us (0.946)
  Pallas kernels: 66.5 us -> 63.1 us
    pallas_call x1, Pallas kernels: 8.8 us -> 6.72 us  [product(): pl.pallas_call(product_kernel, out_shape=jax.ShapeDtypeStruct(((RB_DEV +...]
    pallas_call x1, Pallas kernels: 46 us -> 44.7 us  [gather(): pl.pallas_call(gather_kernel, out_shape=[jax.ShapeDtypeStruct((N_COL, SLA...]
where the time goes in v4:
time: 63.2 us; the launch traced here: 63.1 us
  Pallas kernels  63.1 us (100%)
    pallas_call x1, Pallas kernels, gather(): pl.pallas_call(gather_kernel, out_shape=[jax.ShapeDtypeStruct((N_COL, SLA...  44.7 us
    pallas_call x1, Pallas kernels, column_total(): pl.pallas_call(total_kernel, out_shape=jax.ShapeDtypeStruct(shape, jnp.fl...  7.79 us
    pallas_call x1, Pallas kernels, product(): pl.pallas_call(product_kernel, out_shape=jax.ShapeDtypeStruct(((RB_DEV +...  6.72 us
    pallas_call x1, Pallas kernels, scale(): pl.pallas_call(scale_kernel, out_shape=jax.ShapeDtypeStruct((rows, cols),...  3.89 us

profile of v4, /device:TPU:0, one launch (start us, length us, event | category | flops | bytes accessed | tf_op | source)
XLA Modules:
  0.0 63.1 jit_solution(2037363104799630510)
XLA Ops:
  0.0 44.7 %gather_slabs.1 = (bf16[16,1024,256]{2,1,0:T(8,128)(2,1)S(1)}, bf16[8,1024,256]{2,1,0:T(8,128)(2,1)S(1)}, s32[16,1,128]{2,1,0:T(1,128)S(1)}, s32[8,1,128]{2,1,0:T(1,128)S(1)}) custom-call(bf16[1024,256]{1,0:T(8,128)(2,1)} %bitcast.4, bf16[1024,256]{1,0:T(8,128)(2,1)} %bitcast.5, s32[1,4]{1,0:T(1,128)} %bitcast.6, s32[1,4]{1,0:T(1,128)} %bitcast.7), custom_call_target="tpu_custom_call" | custom-call | tf_op jit(solution)/shard_map/gather_slabs/pallas_call | solution.py:246
  44.7 6.7 %tile_products.1.expanded = f32[36,256,256]{2,1,0:T(8,128)S(1)} custom-call(s32[16,1,128]{2,1,0:T(1,128)S(1)} %get-tuple-element.9.left_ids, s32[8,1,128]{2,1,0:T(1,128)S(1)} %get-tuple-element.10.right_ids, bf16[16,1024,256]{2,1,0:T(8,128)(2,1)S(1)} %get-tuple-element.11.left_all, bf16[8,1024,256]{2,1,0:T(8,128)(2,1)S(1)} %get-tuple-element.12.right_all), custom_call_target="tpu_custom_call" | custom-call | tf_op jit(solution)/shard_map/tile_products/pallas_call | solution.py:300
  51.4 7.8 %column_total.1.total = f32[1,1024]{1,0:T(1,128)S(1)} custom-call(f32[36,256,256]{2,1,0:T(8,128)S(1)} %tile_products.1.expanded), custom_call_target="tpu_custom_call" | custom-call | tf_op jit(solution)/shard_map/column_total/pallas_call | solution.py:345
  59.2 3.9 %scale_columns.1 = f32[2048,1024]{1,0:T(8,128)} custom-call(f32[1,1024]{1,0:T(1,128)S(1)} %column_total.1.total, f32[36,256,256]{2,1,0:T(8,128)S(1)} %tile_products.1.expanded), custom_call_target="tpu_custom_call" | custom-call | tf_op jit(solution)/shard_map/scale_columns/pallas_call | solution.py:383

commit v5 on v4

--- a/solution.py
+++ b/solution.py
@@ -16,6 +16,7 @@
 SLAB = CAP * TILE
 LANES = 128
 EPSILON = 1e-06
+EXPANDED = ((RB_DEV + 1) * CB_DEV, TILE, TILE)
 MESH = pl.DeviceIdType.MESH
 ANY = pl.BlockSpec(memory_space=pl.ANY)
 VMEM = pl.BlockSpec(memory_space=pltpu.VMEM)
@@ -127,7 +128,7 @@
             copy.wait_send()
 
 
-def gather_kernel(left, right, left_slots, right_slots, left_all, right_all, left_ids, right_ids,
+def gather_kernel(left, right, left_slots, right_slots, left_all, right_all, left_ids, right_ids, blank,
                   ids, slots, left_send, left_recv, right_send, right_recv, sib_send, sib_recv,
                   idl_send, idl_recv, idr_send, idr_recv, ids_sib, own_sem):
     row, col = lax.axis_index("row"), lax.axis_index("col")
@@ -209,6 +210,10 @@
     ]
     for copy in local:
         copy.start()
+
+    @pl.loop(0, EXPANDED[0])
+    def _(n):
+        blank[n] = jnp.zeros(EXPANDED[1:], jnp.float32)
 
     slabs = [(ring, pair) for pair in range(2) for ring in range(4)][1:]
     for t in range(2, 14):
@@ -250,9 +255,10 @@
             jax.ShapeDtypeStruct((N_ROW, SLAB, TILE), jnp.bfloat16),
             jax.ShapeDtypeStruct((N_COL, 1, LANES), jnp.int32),
             jax.ShapeDtypeStruct((N_ROW, 1, LANES), jnp.int32),
+            pltpu.VMEM(EXPANDED, jnp.float32),
         ],
         in_specs=[ANY, ANY, ANY, ANY],
-        out_specs=[ANY, ANY, ANY, ANY],
+        out_specs=[ANY, ANY, ANY, ANY, VMEM],
         scratch_shapes=[
             pltpu.VMEM((1, LANES), jnp.int32),
             pltpu.SMEM((2, CAP), jnp.int32),
@@ -268,9 +274,7 @@
 HALF = TILE // 2
 
 
-def product_kernel(left_ids, right_ids, left_all, right_all, expanded):
-    expanded[...] = jnp.zeros_like(expanded)
-
+def product_kernel(left_ids, right_ids, left_all, right_all, blank, expanded):
     def inner(n, _):
         work = []
         for w in range(PER_STEP):
@@ -296,15 +300,16 @@
     lax.fori_loop(0, N_ROW * CAP // PER_STEP, inner, 0)
 
 
-def product(left_ids, right_ids, left_all, right_all):
+def product(left_ids, right_ids, left_all, right_all, blank):
     return pl.pallas_call(
         product_kernel,
-        out_shape=jax.ShapeDtypeStruct(((RB_DEV + 1) * CB_DEV, TILE, TILE), jnp.float32),
-        in_specs=[SMEM, SMEM, VMEM, VMEM],
+        out_shape=pltpu.VMEM(EXPANDED, jnp.float32),
+        in_specs=[SMEM, SMEM, VMEM, VMEM, VMEM],
         out_specs=VMEM,
+        input_output_aliases={4: 0},
         compiler_params=pltpu.CompilerParams(vmem_limit_bytes=4 * 2**20),
         name="tile_products",
-    )(left_ids, right_ids, left_all, right_all)
+    )(left_ids, right_ids, left_all, right_all, blank)
 
 
 def total_kernel(expanded, total, part, held, send, recv):
@@ -355,7 +360,7 @@
     )(expanded)
 
 
-SCALE_ROWS = 128
+SCALE_ROWS = 256
 SCALE_SLOTS = 4
 
 
@@ -386,7 +391,7 @@
         in_specs=[VMEM, VMEM],
         out_specs=ANY,
         scratch_shapes=[pltpu.VMEM((SCALE_SLOTS, SCALE_ROWS, cols), jnp.float32), pltpu.SemaphoreType.DMA((SCALE_SLOTS,))],
-        compiler_params=pltpu.CompilerParams(vmem_limit_bytes=4 * 2**20),
+        compiler_params=pltpu.CompilerParams(vmem_limit_bytes=6 * 2**20),
         name="scale_columns",
     )(total, expanded)
 
@@ -394,10 +399,10 @@
 def body(left_tiles, left_slots, right_tiles, right_slots):
     left = left_tiles.reshape(SLAB, TILE)
     right = right_tiles.reshape(SLAB, TILE)
-    left_all, right_all, left_ids, right_ids = gather(
+    left_all, right_all, left_ids, right_ids, blank = gather(
         left, right, left_slots.reshape(1, CAP), right_slots.reshape(1, CAP)
     )
-    expanded = product(left_ids, right_ids, left_all, right_all)
+    expanded = product(left_ids, right_ids, left_all, right_all, blank)
     return scale(column_total(expanded), expanded)
 
 

time: 63.2 us -> 62.1 us (0.983)
  Pallas kernels: 63.1 us -> 62 us
where the time goes in v5:
time: 62.1 us; the launch traced here: 62 us
  Pallas kernels  62 us (100%)
    pallas_call x1, Pallas kernels, gather(): pl.pallas_call(gather_kernel, out_shape=[jax.ShapeDtypeStruct((N_COL, SLA...  44.7 us
    pallas_call x1, Pallas kernels, column_total(): pl.pallas_call(total_kernel, out_shape=jax.ShapeDtypeStruct(shape, jnp.fl...  7.79 us
    pallas_call x1, Pallas kernels, product(): pl.pallas_call(product_kernel, out_shape=pltpu.VMEM(EXPANDED, jnp.float32...  6.11 us
    pallas_call x1, Pallas kernels, scale(): pl.pallas_call(scale_kernel, out_shape=jax.ShapeDtypeStruct((rows, cols),...  3.42 us

profile of v5, /device:TPU:0, one launch (start us, length us, event | category | flops | bytes accessed | tf_op | source)
XLA Modules:
  0.0 62.0 jit_solution(3553553739917636578)
XLA Ops:
  0.0 44.7 %gather_slabs.1 = (bf16[16,1024,256]{2,1,0:T(8,128)(2,1)S(1)}, bf16[8,1024,256]{2,1,0:T(8,128)(2,1)S(1)}, s32[16,1,128]{2,1,0:T(1,128)S(1)}, s32[8,1,128]{2,1,0:T(1,128)S(1)}, f32[36,256,256]{2,1,0:T(8,128)S(1)}) custom-call(bf16[1024,256]{1,0:T(8,128)(2,1)} %bitcast.4, bf16[1024,256]{1,0:T(8,128)(2,1)} %bitcast.5, s32[1,4]{1,0:T(1,128)} %bitcast.6, ...), custom_call_target="tpu_custom_call" | custom-call | tf_op jit(solution)/shard_map/gather_slabs/pallas_call | solution.py:251
  44.7 6.1 %tile_products.1.expanded = f32[36,256,256]{2,1,0:T(8,128)S(1)} custom-call(s32[16,1,128]{2,1,0:T(1,128)S(1)} %get-tuple-element.10.left_ids, s32[8,1,128]{2,1,0:T(1,128)S(1)} %get-tuple-element.11.right_ids, bf16[16,1024,256]{2,1,0:T(8,128)(2,1)S(1)} %get-tuple-element.12.left_all, ...), custom_call_target="tpu_custom_call", output_to_operand_aliasing={{}: (4, {})} | custom-call | tf_op jit(solution)/shard_map/tile_products/pallas_call | solution.py:304
  50.8 7.8 %column_total.1.total = f32[1,1024]{1,0:T(1,128)S(1)} custom-call(f32[36,256,256]{2,1,0:T(8,128)S(1)} %tile_products.1.expanded), custom_call_target="tpu_custom_call" | custom-call | tf_op jit(solution)/shard_map/column_total/pallas_call | solution.py:350
  58.6 3.4 %scale_columns.1 = f32[2048,1024]{1,0:T(8,128)} custom-call(f32[1,1024]{1,0:T(1,128)S(1)} %column_total.1.total, f32[36,256,256]{2,1,0:T(8,128)S(1)} %tile_products.1.expanded), custom_call_target="tpu_custom_call" | custom-call | tf_op jit(solution)/shard_map/scale_columns/pallas_call | solution.py:388

commit v6 on v5

--- a/solution.py
+++ b/solution.py
@@ -23,7 +23,12 @@
 SMEM = pl.BlockSpec(memory_space=pltpu.SMEM)
 
 
-IDS_ALONG = [("pair", (0, 0)), ("up", (0, 0)), ("up", (3, 0)), ("up", (0, 1)), ("down", (0, 0)), ("down", (0, 1))]
+IDS_TICKS = {
+    1: [((0, 0), 1, 0), ((0, 0), 3, 0), ((0, 0), 0, 1)],
+    3: [((3, 0), 1, 0)],
+    4: [((0, 1), 1, 0), ((0, 1), 3, 0)],
+    6: [((3, 1), 1, 0)],
+}
 PIECES = [(0, TILE), (TILE, TILE), (2 * TILE, TILE), (3 * TILE, TILE), (2 * TILE, TILE // 2), (2 * TILE + TILE // 2, TILE // 2)]
 
 
@@ -45,7 +50,6 @@
         self.send, self.recv, self.sibling = send, recv, sibling
         self.ids_out, self.ids_own, self.ids_place, self.ids_send, self.ids_recv = ids_out, ids_own, ids_place, ids_send, ids_recv
         self.count, self.here, self.ids_here, self.ids_sent = 0, set(), set(), []
-        self.lines_with_ids = {(line, slab) for line, slab in IDS_ALONG}
         self.lines = {"up": [], "down": [], "pair": []}
 
     def tile(self, slab, q):
@@ -70,11 +74,9 @@
         copy.start()
         self.count += 1
         sent.append(copy)
-        if (line, slab) in self.lines_with_ids:
-            self.lines_with_ids.remove((line, slab))
-            self.start_ids(slab, there, ring, pair)
-
-    def start_ids(self, slab, there, ring, pair):
+
+    def start_ids(self, slab, ring, pair):
+        there = ((slab[0] - ring) % 4, (slab[1] - pair) % 2)
         if slab != (0, 0):
             self.ids_arrived(slab)
         copy = pltpu.make_async_remote_copy(
@@ -109,8 +111,8 @@
         if t < len(self.UP):
             self.start("up", *self.UP[t], 1, 0)
             self.start("down", *self.DOWN[t], 3, 0)
-        if t == 8:
-            self.start_ids((3, 1), (2, 1), 1, 0)
+        for way in IDS_TICKS.get(t, ()):
+            self.start_ids(*way)
         if 2 <= t < len(self.UP) + 2:
             (ring, pair), q = self.UP[t - 2]
             self.arrived(((ring + 3) % 4, pair), q)
@@ -155,15 +157,6 @@
         (right_place(1, 0), col), (right_place(3, 0), col), (right_place(0, 1), col),
     ):
         pl.semaphore_signal(barrier, inc=1, device_id=peer, device_id_type=MESH)
-
-    lane = lax.broadcasted_iota(jnp.int32, (1, LANES), 1)
-    for copy in fetch:
-        copy.wait()
-    row_ids = jnp.full((1, LANES), -1, jnp.int32)
-    for s in range(CAP):
-        row_ids = jnp.where(lane == s, slots[0, s], row_ids)
-        row_ids = jnp.where(lane == CAP + s, slots[1, s], row_ids)
-    ids[...] = row_ids
 
     pl.semaphore_wait(barrier, 7)
 
@@ -197,6 +190,16 @@
 
     lf.tick(0)
     rf.tick(0)
+
+    lane = lax.broadcasted_iota(jnp.int32, (1, LANES), 1)
+    for copy in fetch:
+        copy.wait()
+    row_ids = jnp.full((1, LANES), -1, jnp.int32)
+    for s in range(CAP):
+        row_ids = jnp.where(lane == s, slots[0, s], row_ids)
+        row_ids = jnp.where(lane == CAP + s, slots[1, s], row_ids)
+    ids[...] = row_ids
+
     lf.tick(1)
     rf.tick(1)
 
@@ -270,7 +273,7 @@
     )(*operands)
 
 
-PER_STEP = 8
+PER_STEP = 16
 HALF = TILE // 2
 
 
@@ -360,25 +363,26 @@
     )(expanded)
 
 
-SCALE_ROWS = 256
+SCALE_BLOCKS = [TILE // 4, TILE // 4, TILE // 2] + [TILE] * (RB_DEV - 1)
 SCALE_SLOTS = 4
 
 
 def scale_kernel(total, expanded, out, scaled, sems):
     factor = 1.0 / (total[...] / (RB_DEV * TILE * N_ROW) + EPSILON)
-    copies = []
-    for n in range(RB_DEV * TILE // SCALE_ROWS):
+    copies, done = [], 0
+    for n, count in enumerate(SCALE_BLOCKS):
         slot = n % SCALE_SLOTS
         if n >= SCALE_SLOTS:
             copies[n - SCALE_SLOTS].wait()
-        i, first = n * SCALE_ROWS // TILE, n * SCALE_ROWS % TILE
+        i, first = done // TILE, done % TILE
         for j in range(CB_DEV):
             columns = slice(j * TILE, (j + 1) * TILE)
-            value = expanded[i * CB_DEV + j, first : first + SCALE_ROWS]
-            scaled[slot, :, columns] = value * value * factor[:, columns]
-        copy = pltpu.make_async_copy(scaled.at[slot], out.at[pl.ds(n * SCALE_ROWS, SCALE_ROWS)], sems.at[slot])
+            value = expanded[i * CB_DEV + j, first : first + count]
+            scaled[slot, :count, columns] = value * value * factor[:, columns]
+        copy = pltpu.make_async_copy(scaled.at[slot, pl.ds(0, count)], out.at[pl.ds(done, count)], sems.at[slot])
         copy.start()
         copies.append(copy)
+        done += count
     for copy in copies[-SCALE_SLOTS:]:
         copy.wait()
 
@@ -390,7 +394,7 @@
         out_shape=jax.ShapeDtypeStruct((rows, cols), jnp.float32),
         in_specs=[VMEM, VMEM],
         out_specs=ANY,
-        scratch_shapes=[pltpu.VMEM((SCALE_SLOTS, SCALE_ROWS, cols), jnp.float32), pltpu.SemaphoreType.DMA((SCALE_SLOTS,))],
+        scratch_shapes=[pltpu.VMEM((SCALE_SLOTS, TILE, cols), jnp.float32), pltpu.SemaphoreType.DMA((SCALE_SLOTS,))],
         compiler_params=pltpu.CompilerParams(vmem_limit_bytes=6 * 2**20),
         name="scale_columns",
     )(total, expanded)

time: 62.1 us -> 61.9 us (level)
  no operation moved by 1% of the time
where the time goes in v6:
time: 61.9 us; the launch traced here: 61.8 us
  Pallas kernels  61.7 us (100%)
    pallas_call x1, Pallas kernels, gather(): pl.pallas_call(gather_kernel, out_shape=[jax.ShapeDtypeStruct((N_COL, SLA...  44.7 us
    pallas_call x1, Pallas kernels, column_total(): pl.pallas_call(total_kernel, out_shape=jax.ShapeDtypeStruct(shape, jnp.fl...  7.79 us
    pallas_call x1, Pallas kernels, product(): pl.pallas_call(product_kernel, out_shape=pltpu.VMEM(EXPANDED, jnp.float32...  5.8 us
    pallas_call x1, Pallas kernels, scale(): pl.pallas_call(scale_kernel, out_shape=jax.ShapeDtypeStruct((rows, cols),...  3.45 us

profile of v6, /device:TPU:0, one launch (start us, length us, event | category | flops | bytes accessed | tf_op | source)
XLA Modules:
  0.0 61.8 jit_solution(1767760935306099423)
XLA Ops:
  0.0 44.7 %gather_slabs.1 = (bf16[16,1024,256]{2,1,0:T(8,128)(2,1)S(1)}, bf16[8,1024,256]{2,1,0:T(8,128)(2,1)S(1)}, s32[16,1,128]{2,1,0:T(1,128)S(1)}, s32[8,1,128]{2,1,0:T(1,128)S(1)}, f32[36,256,256]{2,1,0:T(8,128)S(1)}) custom-call(bf16[1024,256]{1,0:T(8,128)(2,1)} %bitcast.4, bf16[1024,256]{1,0:T(8,128)(2,1)} %bitcast.5, s32[1,4]{1,0:T(1,128)} %bitcast.6, ...), custom_call_target="tpu_custom_call" | custom-call | tf_op jit(solution)/shard_map/gather_slabs/pallas_call | solution.py:254
  44.7 5.8 %tile_products.1.expanded = f32[36,256,256]{2,1,0:T(8,128)S(1)} custom-call(s32[16,1,128]{2,1,0:T(1,128)S(1)} %get-tuple-element.10.left_ids, s32[8,1,128]{2,1,0:T(1,128)S(1)} %get-tuple-element.11.right_ids, bf16[16,1024,256]{2,1,0:T(8,128)(2,1)S(1)} %get-tuple-element.12.left_all, ...), custom_call_target="tpu_custom_call", output_to_operand_aliasing={{}: (4, {})} | custom-call | tf_op jit(solution)/shard_map/tile_products/pallas_call | solution.py:307
  50.5 7.8 %column_total.1.total = f32[1,1024]{1,0:T(1,128)S(1)} custom-call(f32[36,256,256]{2,1,0:T(8,128)S(1)} %tile_products.1.expanded), custom_call_target="tpu_custom_call" | custom-call | tf_op jit(solution)/shard_map/column_total/pallas_call | solution.py:353
  58.3 3.5 %scale_columns.1 = f32[2048,1024]{1,0:T(8,128)} custom-call(f32[1,1024]{1,0:T(1,128)S(1)} %column_total.1.total, f32[36,256,256]{2,1,0:T(8,128)S(1)} %tile_products.1.expanded), custom_call_target="tpu_custom_call" | custom-call | tf_op jit(solution)/shard_map/scale_columns/pallas_call | solution.py:392

commit v7 on v6

--- a/solution.py
+++ b/solution.py
@@ -130,7 +130,7 @@
             copy.wait_send()
 
 
-def gather_kernel(left, right, left_slots, right_slots, left_all, right_all, left_ids, right_ids, blank,
+def gather_kernel(left, right, left_slots, right_slots, left_all, right_all, all_ids, blank,
                   ids, slots, left_send, left_recv, right_send, right_recv, sib_send, sib_recv,
                   idl_send, idl_recv, idr_send, idr_recv, ids_sib, own_sem):
     row, col = lax.axis_index("row"), lax.axis_index("col")
@@ -181,11 +181,11 @@
 
     lf = Factor(
         left_all, left, left_place, lambda ring, pair: (row, left_place(ring, pair)), left_send, left_recv, to_sibling,
-        left_ids, ids, left_ids_place, idl_send, idl_recv, (2, 3),
+        all_ids, ids, left_ids_place, idl_send, idl_recv, (2, 3),
     )
     rf = Factor(
         right_all, right, right_place, lambda ring, pair: (right_place(ring, pair), col), right_send, right_recv, None,
-        right_ids, ids, right_place, idr_send, idr_recv, (3,),
+        all_ids, ids, lambda ring, pair: N_COL + right_place(ring, pair), idr_send, idr_recv, (3,),
     )
 
     lf.tick(0)
@@ -208,8 +208,8 @@
     local = [
         pltpu.make_async_copy(left, left_all.at[col], own_sem.at[0]),
         pltpu.make_async_copy(right, right_all.at[row], own_sem.at[1]),
-        pltpu.make_async_copy(ids, left_ids.at[left_ids_place(0, 0)], own_sem.at[2]),
-        pltpu.make_async_copy(ids, right_ids.at[row], own_sem.at[3]),
+        pltpu.make_async_copy(ids, all_ids.at[left_ids_place(0, 0)], own_sem.at[2]),
+        pltpu.make_async_copy(ids, all_ids.at[N_COL + row], own_sem.at[3]),
     ]
     for copy in local:
         copy.start()
@@ -221,12 +221,12 @@
     slabs = [(ring, pair) for pair in range(2) for ring in range(4)][1:]
     for t in range(2, 14):
         lf.tick(t)
-        if t == 12:
+        if t == 10:
             for copy in local:
                 copy.wait()
             for slab in slabs:
                 lf.ids_arrived(slab)
-            block = left_ids.at[pl.ds(core * N_ROW, N_ROW)]
+            block = all_ids.at[pl.ds(core * N_ROW, N_ROW)]
             copy = pltpu.make_async_remote_copy(
                 src_ref=block, dst_ref=block, send_sem=ids_sib.at[0], recv_sem=ids_sib.at[1], device_id=other, device_id_type=MESH)
             copy.start()
@@ -240,7 +240,7 @@
         place = left_place(ring, pair) + 1 - 2 * core
         part = left_all.at[place, pl.ds(q * TILE, TILE)]
         pltpu.make_async_copy(part, part, sib_recv.at[index]).wait()
-    theirs = left_ids.at[pl.ds((1 - core) * N_ROW, N_ROW)]
+    theirs = all_ids.at[pl.ds((1 - core) * N_ROW, N_ROW)]
     pltpu.make_async_copy(theirs, theirs, ids_sib.at[1]).wait()
     for copy in shared:
         copy.wait_send()
@@ -256,12 +256,11 @@
         out_shape=[
             jax.ShapeDtypeStruct((N_COL, SLAB, TILE), jnp.bfloat16),
             jax.ShapeDtypeStruct((N_ROW, SLAB, TILE), jnp.bfloat16),
-            jax.ShapeDtypeStruct((N_COL, 1, LANES), jnp.int32),
-            jax.ShapeDtypeStruct((N_ROW, 1, LANES), jnp.int32),
+            jax.ShapeDtypeStruct((N_COL + N_ROW, 1, LANES), jnp.int32),
             pltpu.VMEM(EXPANDED, jnp.float32),
         ],
         in_specs=[ANY, ANY, ANY, ANY],
-        out_specs=[ANY, ANY, ANY, ANY, VMEM],
+        out_specs=[ANY, ANY, ANY, VMEM],
         scratch_shapes=[
             pltpu.VMEM((1, LANES), jnp.int32),
             pltpu.SMEM((2, CAP), jnp.int32),
@@ -277,18 +276,18 @@
 HALF = TILE // 2
 
 
-def product_kernel(left_ids, right_ids, left_all, right_all, blank, expanded):
+def product_kernel(all_ids, left_all, right_all, blank, expanded):
     def inner(n, _):
         work = []
         for w in range(PER_STEP):
             q, s = n * (PER_STEP // CAP) + w // CAP, w % CAP
-            held = right_ids[q, 0, CAP + s]
+            held = all_ids[N_COL + q, 0, CAP + s]
             kept = held >= 0
             held = jnp.where(kept, held, 0)
             parity = held // CB_DEV
             rows = []
             for u in range(CAP):
-                i = left_ids[parity * N_ROW + q, 0, u]
+                i = all_ids[parity * N_ROW + q, 0, u]
                 rows.append(jnp.where(kept & (i >= 0), i, RB_DEV))
             work.append((q, s, 2 * q + parity, lax.rem(held, CB_DEV), rows))
         for q, s, k, j, rows in work:
@@ -303,16 +302,16 @@
     lax.fori_loop(0, N_ROW * CAP // PER_STEP, inner, 0)
 
 
-def product(left_ids, right_ids, left_all, right_all, blank):
+def product(all_ids, left_all, right_all, blank):
     return pl.pallas_call(
         product_kernel,
         out_shape=pltpu.VMEM(EXPANDED, jnp.float32),
-        in_specs=[SMEM, SMEM, VMEM, VMEM, VMEM],
+        in_specs=[SMEM, VMEM, VMEM, VMEM],
         out_specs=VMEM,
-        input_output_aliases={4: 0},
+        input_output_aliases={3: 0},
         compiler_params=pltpu.CompilerParams(vmem_limit_bytes=4 * 2**20),
         name="tile_products",
-    )(left_ids, right_ids, left_all, right_all, blank)
+    )(all_ids, left_all, right_all, blank)
 
 
 def total_kernel(expanded, total, part, held, send, recv):
@@ -363,7 +362,7 @@
     )(expanded)
 
 
-SCALE_BLOCKS = [TILE // 4, TILE // 4, TILE // 2] + [TILE] * (RB_DEV - 1)
+SCALE_BLOCKS = [TILE] * RB_DEV
 SCALE_SLOTS = 4
 
 
@@ -403,10 +402,10 @@
 def body(left_tiles, left_slots, right_tiles, right_slots):
     left = left_tiles.reshape(SLAB, TILE)
     right = right_tiles.reshape(SLAB, TILE)
-    left_all, right_all, left_ids, right_ids, blank = gather(
+    left_all, right_all, all_ids, blank = gather(
         left, right, left_slots.reshape(1, CAP), right_slots.reshape(1, CAP)
     )
-    expanded = product(left_ids, right_ids, left_all, right_all, blank)
+    expanded = product(all_ids, left_all, right_all, blank)
     return scale(column_total(expanded), expanded)
 
 

time: 61.9 us -> 61.8 us (level)
  no operation moved by 1% of the time
where the time goes in v7:
time: 61.8 us; the launch traced here: 61.7 us
  Pallas kernels  61.7 us (100%)
    pallas_call x1, Pallas kernels, gather(): pl.pallas_call(gather_kernel, out_shape=[jax.ShapeDtypeStruct((N_COL, SLA...  44.7 us
    pallas_call x1, Pallas kernels, column_total(): pl.pallas_call(total_kernel, out_shape=jax.ShapeDtypeStruct(shape, jnp.fl...  7.79 us
    pallas_call x1, Pallas kernels, product(): pl.pallas_call(product_kernel, out_shape=pltpu.VMEM(EXPANDED, jnp.float32...  5.81 us
    pallas_call x1, Pallas kernels, scale(): pl.pallas_call(scale_kernel, out_shape=jax.ShapeDtypeStruct((rows, cols),...  3.42 us

profile of v7, /device:TPU:0, one launch (start us, length us, event | category | flops | bytes accessed | tf_op | source)
XLA Modules:
  0.0 61.7 jit_solution(4095106733518819412)
XLA Ops:
  0.0 44.7 %gather_slabs.1 = (bf16[16,1024,256]{2,1,0:T(8,128)(2,1)S(1)}, bf16[8,1024,256]{2,1,0:T(8,128)(2,1)S(1)}, s32[24,1,128]{2,1,0:T(1,128)S(1)}, f32[36,256,256]{2,1,0:T(8,128)S(1)}) custom-call(bf16[1024,256]{1,0:T(8,128)(2,1)} %bitcast.4, bf16[1024,256]{1,0:T(8,128)(2,1)} %bitcast.5, s32[1,4]{1,0:T(1,128)} %bitcast.6, s32[1,4]{1,0:T(1,128)} %bitcast.7), custom_call_target="tpu_custom_call" | custom-call | tf_op jit(solution)/shard_map/gather_slabs/pallas_call | solution.py:254
  44.7 5.8 %tile_products.1.expanded = f32[36,256,256]{2,1,0:T(8,128)S(1)} custom-call(s32[24,1,128]{2,1,0:T(1,128)S(1)} %get-tuple-element.9.all_ids, bf16[16,1024,256]{2,1,0:T(8,128)(2,1)S(1)} %get-tuple-element.10.left_all, bf16[8,1024,256]{2,1,0:T(8,128)(2,1)S(1)} %get-tuple-element.11.right_all, ...), custom_call_target="tpu_custom_call", output_to_operand_aliasing={{}: (3, {})} | custom-call | tf_op jit(solution)/shard_map/tile_products/pallas_call | solution.py:306
  50.5 7.8 %column_total.1.total = f32[1,1024]{1,0:T(1,128)S(1)} custom-call(f32[36,256,256]{2,1,0:T(8,128)S(1)} %tile_products.1.expanded), custom_call_target="tpu_custom_call" | custom-call | tf_op jit(solution)/shard_map/column_total/pallas_call | solution.py:352
  58.3 3.4 %scale_columns.1 = f32[2048,1024]{1,0:T(8,128)} custom-call(f32[1,1024]{1,0:T(1,128)S(1)} %column_total.1.total, f32[36,256,256]{2,1,0:T(8,128)S(1)} %tile_products.1.expanded), custom_call_target="tpu_custom_call" | custom-call | tf_op jit(solution)/shard_map/scale_columns/pallas_call | solution.py:391

commit v8 on v7

--- a/solution.py
+++ b/solution.py
@@ -33,7 +33,7 @@
 
 
 class Factor:
-    WINDOW = 2
+    WINDOW = 3
 
     def __init__(self, out, own, place, device, send, recv, sibling, ids_out, ids_own, ids_place, ids_send, ids_recv, across):
         self.across = across

time: 61.8 us -> 61.8 us (level)
  no operation moved by 1% of the time
where the time goes in v8:
time: 61.8 us; the launch traced here: 61.7 us
  Pallas kernels  61.7 us (100%)
    pallas_call x1, Pallas kernels, gather(): pl.pallas_call(gather_kernel, out_shape=[jax.ShapeDtypeStruct((N_COL, SLA...  44.7 us
    pallas_call x1, Pallas kernels, column_total(): pl.pallas_call(total_kernel, out_shape=jax.ShapeDtypeStruct(shape, jnp.fl...  7.79 us
    pallas_call x1, Pallas kernels, product(): pl.pallas_call(product_kernel, out_shape=pltpu.VMEM(EXPANDED, jnp.float32...  5.8 us
    pallas_call x1, Pallas kernels, scale(): pl.pallas_call(scale_kernel, out_shape=jax.ShapeDtypeStruct((rows, cols),...  3.42 us

profile of v8, /device:TPU:0, one launch (start us, length us, event | category | flops | bytes accessed | tf_op | source)
XLA Modules:
  0.0 61.7 jit_solution(12760426815686998692)
XLA Ops:
  0.0 44.7 %gather_slabs.1 = (bf16[16,1024,256]{2,1,0:T(8,128)(2,1)S(1)}, bf16[8,1024,256]{2,1,0:T(8,128)(2,1)S(1)}, s32[24,1,128]{2,1,0:T(1,128)S(1)}, f32[36,256,256]{2,1,0:T(8,128)S(1)}) custom-call(bf16[1024,256]{1,0:T(8,128)(2,1)} %bitcast.4, bf16[1024,256]{1,0:T(8,128)(2,1)} %bitcast.5, s32[1,4]{1,0:T(1,128)} %bitcast.6, s32[1,4]{1,0:T(1,128)} %bitcast.7), custom_call_target="tpu_custom_call" | custom-call | tf_op jit(solution)/shard_map/gather_slabs/pallas_call | solution.py:254
  44.7 5.8 %tile_products.1.expanded = f32[36,256,256]{2,1,0:T(8,128)S(1)} custom-call(s32[24,1,128]{2,1,0:T(1,128)S(1)} %get-tuple-element.9.all_ids, bf16[16,1024,256]{2,1,0:T(8,128)(2,1)S(1)} %get-tuple-element.10.left_all, bf16[8,1024,256]{2,1,0:T(8,128)(2,1)S(1)} %get-tuple-element.11.right_all, ...), custom_call_target="tpu_custom_call", output_to_operand_aliasing={{}: (3, {})} | custom-call | tf_op jit(solution)/shard_map/tile_products/pallas_call | solution.py:306
  50.5 7.8 %column_total.1.total = f32[1,1024]{1,0:T(1,128)S(1)} custom-call(f32[36,256,256]{2,1,0:T(8,128)S(1)} %tile_products.1.expanded), custom_call_target="tpu_custom_call" | custom-call | tf_op jit(solution)/shard_map/column_total/pallas_call | solution.py:352
  58.3 3.4 %scale_columns.1 = f32[2048,1024]{1,0:T(8,128)} custom-call(f32[1,1024]{1,0:T(1,128)S(1)} %column_total.1.total, f32[36,256,256]{2,1,0:T(8,128)S(1)} %tile_products.1.expanded), custom_call_target="tpu_custom_call" | custom-call | tf_op jit(solution)/shard_map/scale_columns/pallas_call | solution.py:391

commit v9 on v7

--- a/solution.py
+++ b/solution.py
@@ -272,7 +272,7 @@
     )(*operands)
 
 
-PER_STEP = 16
+PER_STEP = 8
 HALF = TILE // 2
 
 
@@ -363,7 +363,7 @@
 
 
 SCALE_BLOCKS = [TILE] * RB_DEV
-SCALE_SLOTS = 4
+SCALE_SLOTS = 8
 
 
 def scale_kernel(total, expanded, out, scaled, sems):
@@ -394,7 +394,7 @@
         in_specs=[VMEM, VMEM],
         out_specs=ANY,
         scratch_shapes=[pltpu.VMEM((SCALE_SLOTS, TILE, cols), jnp.float32), pltpu.SemaphoreType.DMA((SCALE_SLOTS,))],
-        compiler_params=pltpu.CompilerParams(vmem_limit_bytes=6 * 2**20),
+        compiler_params=pltpu.CompilerParams(vmem_limit_bytes=10 * 2**20),
         name="scale_columns",
     )(total, expanded)
 

time: 61.8 us -> 62.2 us (level)
  no operation moved by 1% of the time
where the time goes in v9:
time: 62.2 us; the launch traced here: 62.1 us
  Pallas kernels  62.1 us (100%)
    pallas_call x1, Pallas kernels, gather(): pl.pallas_call(gather_kernel, out_shape=[jax.ShapeDtypeStruct((N_COL, SLA...  44.7 us
    pallas_call x1, Pallas kernels, column_total(): pl.pallas_call(total_kernel, out_shape=jax.ShapeDtypeStruct(shape, jnp.fl...  7.79 us
    pallas_call x1, Pallas kernels, product(): pl.pallas_call(product_kernel, out_shape=pltpu.VMEM(EXPANDED, jnp.float32...  6.16 us
    pallas_call x1, Pallas kernels, scale(): pl.pallas_call(scale_kernel, out_shape=jax.ShapeDtypeStruct((rows, cols),...  3.46 us

profile of v9, /device:TPU:0, one launch (start us, length us, event | category | flops | bytes accessed | tf_op | source)
XLA Modules:
  0.0 62.1 jit_solution(5275566303293187439)
XLA Ops:
  0.0 44.7 %gather_slabs.1 = (bf16[16,1024,256]{2,1,0:T(8,128)(2,1)S(1)}, bf16[8,1024,256]{2,1,0:T(8,128)(2,1)S(1)}, s32[24,1,128]{2,1,0:T(1,128)S(1)}, f32[36,256,256]{2,1,0:T(8,128)S(1)}) custom-call(bf16[1024,256]{1,0:T(8,128)(2,1)} %bitcast.4, bf16[1024,256]{1,0:T(8,128)(2,1)} %bitcast.5, s32[1,4]{1,0:T(1,128)} %bitcast.6, s32[1,4]{1,0:T(1,128)} %bitcast.7), custom_call_target="tpu_custom_call" | custom-call | tf_op jit(solution)/shard_map/gather_slabs/pallas_call | solution.py:254
  44.7 6.2 %tile_products.1.expanded = f32[36,256,256]{2,1,0:T(8,128)S(1)} custom-call(s32[24,1,128]{2,1,0:T(1,128)S(1)} %get-tuple-element.9.all_ids, bf16[16,1024,256]{2,1,0:T(8,128)(2,1)S(1)} %get-tuple-element.10.left_all, bf16[8,1024,256]{2,1,0:T(8,128)(2,1)S(1)} %get-tuple-element.11.right_all, ...), custom_call_target="tpu_custom_call", output_to_operand_aliasing={{}: (3, {})} | custom-call | tf_op jit(solution)/shard_map/tile_products/pallas_call | solution.py:306
  50.9 7.8 %column_total.1.total = f32[1,1024]{1,0:T(1,128)S(1)} custom-call(f32[36,256,256]{2,1,0:T(8,128)S(1)} %tile_products.1.expanded), custom_call_target="tpu_custom_call" | custom-call | tf_op jit(solution)/shard_map/column_total/pallas_call | solution.py:352
  58.7 3.5 %scale_columns.1 = f32[2048,1024]{1,0:T(8,128)} custom-call(f32[1,1024]{1,0:T(1,128)S(1)} %column_total.1.total, f32[36,256,256]{2,1,0:T(8,128)S(1)} %tile_products.1.expanded), custom_call_target="tpu_custom_call" | custom-call | tf_op jit(solution)/shard_map/scale_columns/pallas_call | solution.py:391
